TPU v7x, 32 devices: a whole 2x2x4 slice. The times are simulated.
32 devices in a mesh: dp: 4 (over y, x), seq: 8 (over z, core).
Axes of the slice: x: 2, y: 2, z: 4, core: 2. Of those that a mesh axis runs over, the one named last changes fastest.
Arguments:
- hidden_in: bfloat16 [8, 1024, 896], P('dp', 'seq'), may hold values from -6 to 6
- segments: int32 [8, 1024], P('dp', 'seq'), may hold values from 0 to 3, as said below
- w_query: bfloat16 [802816], P(('dp', 'seq')), may hold values from -0.25 to 0.25
- w_key: bfloat16 [114688], P(('dp', 'seq')), may hold values from -0.25 to 0.25
- w_value: bfloat16 [114688], P(('dp', 'seq')), may hold values from -0.1875 to 0.1875
- w_out: bfloat16 [802816], P(('dp', 'seq')), may hold values from -0.75 to 0.75
- w_gate: bfloat16 [4358144], P(('dp', 'seq')), may hold values from -0.1875 to 0.1875
- w_up: bfloat16 [4358144], P(('dp', 'seq')), may hold values from -0.1875 to 0.1875
- w_down: bfloat16 [4358144], P(('dp', 'seq')), may hold values from -0.15625 to 0.15625
- gain_vector: bfloat16 [1792], P('seq'), may hold values from 0.099609375 to 1.8984375
- bias_vector: bfloat16 [1152], P('seq'), may hold values from -3 to 3
- out_grad: bfloat16 [8, 1024, 896], P('dp', 'seq'), may hold values from -6 to 6
Outputs:
- output: bfloat16 [8, 1024, 896], P('dp', 'seq')
- input_grad: float32 [8, 1024, 896], P('dp', 'seq')
- grad_query: float32 [802816], P(('dp', 'seq'))
- grad_key: float32 [114688], P(('dp', 'seq'))
- grad_value: float32 [114688], P(('dp', 'seq'))
- grad_out: float32 [802816], P(('dp', 'seq'))
- grad_gate: float32 [4358144], P(('dp', 'seq'))
- grad_up: float32 [4358144], P(('dp', 'seq'))
- grad_down: float32 [4358144], P(('dp', 'seq'))
- gain_grad: float32 [1792], P('seq')
- bias_grad: float32 [1152], P('seq')
Inputs may be any that keep to these rules, and one draw needn't show every extreme that they name: `segments`: segment numbers start at 0 and never fall along a sequence. Of the 2 sequences of each dp index one, drawn from the seed, is a single document of 1024 tokens; every other sequence holds exactly 4 documents, each of 128 tokens or more.
All inputs are finite; a program needn't handle non-finite values.
Results may differ from a plain program's by a relative error of at most 0.015.
The roundings to bfloat16 on the way count: a program that leaves them out, or rounds other values in their place, can miss the bound.
Values may be sent and summed in bfloat16 or wider, within the bound.
A program may use at most 256 MiB of HBM per device.

v0:
```python
import math

import jax
import jax.numpy as jnp
from jax import lax
from jax.sharding import PartitionSpec as P

D = 896
HEADS = 14
KVH = 2
HD = 64
FF = 4864
KVW = 128
DOCS = 4


EPSILON = 1e-06
ROPE_BASE = 1000000.0
MASKED = -1e30


def rms_norm(values, scaling):
    return values * lax.rsqrt(jnp.mean(values * values, axis=-1, keepdims=True) + EPSILON) * scaling


def rope_tables(places, head_size):
    half = head_size // 2
    freqs = jnp.exp(jnp.arange(half).astype(jnp.float32) * (-2.0 * math.log(ROPE_BASE) / head_size))
    angles = places.astype(jnp.float32)[..., None] * freqs
    cosine = jnp.cos(angles)
    sine = jnp.sin(angles)
    return (jnp.concatenate([cosine, cosine], axis=-1), jnp.concatenate([sine, sine], axis=-1))


def turn(values, cosine, sine):
    half = values.shape[-1] // 2
    turned = jnp.concatenate([-values[..., half:], values[..., :half]], axis=-1)
    return values * cosine + turned * sine


def unturn(gradient, cosine, sine):
    half = gradient.shape[-1] // 2
    scaled = gradient * sine
    return gradient * cosine + jnp.concatenate([scaled[..., half:], -scaled[..., :half]], axis=-1)


def doc_places(doc_ids):
    length = doc_ids.shape[-1]
    numbers = jnp.arange(DOCS)
    starts = jnp.sum((doc_ids[..., :, None] < numbers).astype(jnp.int32), axis=-2)
    first_index = jnp.sum(
        jnp.where(doc_ids[..., :, None] == numbers, starts[..., None, :], 0), axis=-1
    )
    return jnp.arange(length) - first_index


def gated(gate_part, up_part):
    return jax.nn.silu(gate_part) * up_part


def matmul(left, right):
    return jnp.dot(left, right, preferred_element_type=jnp.float32)


def contract_last(left, right):
    return lax.dot_general(
        left, right, (((1,), (1,)), ((), ())), preferred_element_type=jnp.float32
    )


def contract_first(left, right):
    return lax.dot_general(
        left, right, (((0,), (0,)), ((), ())), preferred_element_type=jnp.float32
    )


def unflatten(pieces):
    return (
        pieces[0].reshape(D, D),
        pieces[1].reshape(D, KVW),
        pieces[2].reshape(D, KVW),
        pieces[3].reshape(D, D),
        pieces[4].reshape(D, FF),
        pieces[5].reshape(D, FF),
        pieces[6].reshape(FF, D),
    )


def masked_scores(queries, key_rows, allowed):
    scores = jnp.einsum(
        "hgqd,hld->hgql", queries, key_rows, preferred_element_type=jnp.float32
    ) * HD ** (-0.5)
    return jnp.where(allowed, scores, MASKED)


def attend_forward(pieces):
    queries, key_rows, values, allowed = pieces
    scores = masked_scores(queries, key_rows, allowed)
    highest = jnp.max(scores, axis=-1, keepdims=True)
    weights = jnp.exp(scores - highest)
    summed = jnp.sum(weights, axis=-1, keepdims=True)
    shares = (weights / summed).astype(jnp.bfloat16)
    mixed_heads = jnp.einsum("hgql,hld->hgqd", shares, values, preferred_element_type=jnp.float32)
    return (mixed_heads, (highest + jnp.log(summed))[..., 0])


def attend_backward(pieces):
    queries, key_rows, values, allowed, log_total, grad_mixed = pieces
    scores = masked_scores(queries, key_rows, allowed)
    shares = jnp.exp(scores - log_total[..., None])
    shares_low = shares.astype(jnp.bfloat16)
    grad_shares = jnp.einsum(
        "hgqd,hld->hgql", grad_mixed, values, preferred_element_type=jnp.float32
    )
    inner = jnp.sum(shares * grad_shares, axis=-1, keepdims=True)
    grad_scores = (shares * (grad_shares - inner)).astype(jnp.bfloat16)
    score_scale = HD ** (-0.5)
    grad_queries = (
        jnp.einsum("hgql,hld->hgqd", grad_scores, key_rows, preferred_element_type=jnp.float32)
        * score_scale
    )
    grad_keys = (
        jnp.einsum("hgql,hgqd->hld", grad_scores, queries, preferred_element_type=jnp.float32)
        * score_scale
    )
    grad_values = jnp.einsum(
        "hgql,hgqd->hld", shares_low, grad_mixed, preferred_element_type=jnp.float32
    )
    return (grad_queries, grad_keys, grad_values)


def shards(
    hidden_in,
    segments,
    w_query,
    w_key,
    w_value,
    w_out,
    w_gate,
    w_up,
    w_down,
    gain_vector,
    bias_vector,
    out_grad,
):
    seq_count = hidden_in.shape[0]
    block_len = hidden_in.shape[1]
    seq_len = block_len * lax.axis_size("seq")
    offset = lax.axis_index("seq") * block_len
    row_count = seq_count * block_len
    group_size = HEADS // KVH
    weights = unflatten(
        (
            lax.all_gather(w_query, ("dp", "seq"), axis=0, tiled=True),
            lax.all_gather(w_key, ("dp", "seq"), axis=0, tiled=True),
            lax.all_gather(w_value, ("dp", "seq"), axis=0, tiled=True),
            lax.all_gather(w_out, ("dp", "seq"), axis=0, tiled=True),
            lax.all_gather(w_gate, ("dp", "seq"), axis=0, tiled=True),
            lax.all_gather(w_up, ("dp", "seq"), axis=0, tiled=True),
            lax.all_gather(w_down, ("dp", "seq"), axis=0, tiled=True),
        )
    )
    query_mat, key_mat, value_mat, out_mat, gate_mat, up_mat, down_mat = weights
    gain_full, bias_full = (
        lax.all_gather(gain_vector, "seq", axis=0, tiled=True),
        lax.all_gather(bias_vector, "seq", axis=0, tiled=True),
    )
    first_gain = gain_full[:D].astype(jnp.float32)
    second_gain = gain_full[D:].astype(jnp.float32)
    bias_wide = bias_full.astype(jnp.float32)
    doc_all = lax.all_gather(segments, "seq", axis=1, tiled=True)
    places_all = doc_places(doc_all)
    cos_all, sin_all = rope_tables(places_all, HD)
    cos_here = lax.dynamic_slice_in_dim(cos_all, offset, block_len, 1)
    sin_here = lax.dynamic_slice_in_dim(sin_all, offset, block_len, 1)
    key_index = jnp.arange(seq_len)
    query_index = offset + jnp.arange(block_len)
    allowed = (segments[:, :, None] == doc_all[:, None, :]) & (
        key_index[None, None, :] <= query_index[None, :, None]
    )
    inputs = hidden_in.astype(jnp.float32).reshape(row_count, D)
    normed = rms_norm(inputs, first_gain).astype(jnp.bfloat16)
    query_pre = matmul(normed, query_mat) + bias_wide[:D]
    key_low = (
        (matmul(normed, key_mat) + bias_wide[D : D + KVW])
        .astype(jnp.bfloat16)
        .reshape(seq_count, block_len, KVW)
    )
    value_low = (
        (matmul(normed, value_mat) + bias_wide[D + KVW :])
        .astype(jnp.bfloat16)
        .reshape(seq_count, block_len, KVW)
    )
    key_all, value_all = (
        lax.all_gather(key_low, "seq", axis=1, tiled=True),
        lax.all_gather(value_low, "seq", axis=1, tiled=True),
    )
    key_heads = (
        key_all.astype(jnp.float32).reshape(seq_count, seq_len, KVH, HD).transpose(0, 2, 1, 3)
    )
    key_rot = turn(key_heads, cos_all[:, None], sin_all[:, None]).astype(jnp.bfloat16)
    value_heads = value_all.reshape(seq_count, seq_len, KVH, HD).transpose(0, 2, 1, 3)
    query_heads = query_pre.reshape(seq_count, block_len, KVH, group_size, HD).transpose(
        0, 2, 3, 1, 4
    )
    query_rot = turn(query_heads, cos_here[:, None, None], sin_here[:, None, None]).astype(
        jnp.bfloat16
    )
    mixed_heads, log_total = lax.map(attend_forward, (query_rot, key_rot, value_heads, allowed))
    mixed_rows = mixed_heads.transpose(0, 3, 1, 2, 4).reshape(row_count, D).astype(jnp.bfloat16)
    middle = inputs + matmul(mixed_rows, out_mat)
    normed_two = rms_norm(middle, second_gain).astype(jnp.bfloat16)
    gate_pre = matmul(normed_two, gate_mat)
    up_pre = matmul(normed_two, up_mat)
    activated = gated(gate_pre, up_pre).astype(jnp.bfloat16)
    result = middle + matmul(activated, down_mat)
    output = result.astype(jnp.bfloat16).reshape(seq_count, block_len, D)
    back_weights = unflatten(
        (
            lax.all_gather(w_query, ("dp", "seq"), axis=0, tiled=True),
            lax.all_gather(w_key, ("dp", "seq"), axis=0, tiled=True),
            lax.all_gather(w_value, ("dp", "seq"), axis=0, tiled=True),
            lax.all_gather(w_out, ("dp", "seq"), axis=0, tiled=True),
            lax.all_gather(w_gate, ("dp", "seq"), axis=0, tiled=True),
            lax.all_gather(w_up, ("dp", "seq"), axis=0, tiled=True),
            lax.all_gather(w_down, ("dp", "seq"), axis=0, tiled=True),
        )
    )
    query_mat, key_mat, value_mat, out_mat, gate_mat, up_mat, down_mat = back_weights
    grad_result = out_grad.astype(jnp.float32).reshape(row_count, D)
    grad_branch = grad_result.astype(jnp.bfloat16)
    grad_down_mat = contract_first(activated, grad_branch)
    grad_act = contract_last(grad_branch, down_mat)
    grad_gate_pre, grad_up_pre = jax.vjp(gated, gate_pre, up_pre)[1](grad_act)
    grad_gate_low = grad_gate_pre.astype(jnp.bfloat16)
    grad_up_low = grad_up_pre.astype(jnp.bfloat16)
    grad_gate_mat = contract_first(normed_two, grad_gate_low)
    grad_up_mat = contract_first(normed_two, grad_up_low)
    grad_normed_two = contract_last(grad_gate_low, gate_mat) + contract_last(grad_up_low, up_mat)
    grad_middle_part, grad_second_gain = jax.vjp(rms_norm, middle, second_gain)[1](grad_normed_two)
    grad_middle = grad_result + grad_middle_part
    grad_attn = grad_middle.astype(jnp.bfloat16)
    grad_out_mat = contract_first(mixed_rows, grad_attn)
    grad_mixed = contract_last(grad_attn, out_mat).astype(jnp.bfloat16)
    grad_mixed = grad_mixed.reshape(seq_count, block_len, KVH, group_size, HD).transpose(
        0, 2, 3, 1, 4
    )
    grad_query_rot, grad_key_rot, grad_value_heads = lax.map(
        attend_backward, (query_rot, key_rot, value_heads, allowed, log_total, grad_mixed)
    )
    grad_query_pre = unturn(grad_query_rot, cos_here[:, None, None], sin_here[:, None, None])
    grad_query_low = (
        grad_query_pre.transpose(0, 3, 1, 2, 4).reshape(row_count, D).astype(jnp.bfloat16)
    )
    grad_key_all = (
        unturn(grad_key_rot, cos_all[:, None], sin_all[:, None])
        .transpose(0, 2, 1, 3)
        .reshape(seq_count, seq_len, KVW)
    )
    grad_value_all = grad_value_heads.transpose(0, 2, 1, 3).reshape(seq_count, seq_len, KVW)
    grad_key_sum, grad_value_sum = (
        lax.psum_scatter(
            grad_key_all.astype(jnp.bfloat16), "seq", scatter_dimension=1, tiled=True
        ).astype(jnp.float32),
        lax.psum_scatter(
            grad_value_all.astype(jnp.bfloat16), "seq", scatter_dimension=1, tiled=True
        ).astype(jnp.float32),
    )
    grad_key_low = grad_key_sum.reshape(row_count, KVW).astype(jnp.bfloat16)
    grad_value_low = grad_value_sum.reshape(row_count, KVW).astype(jnp.bfloat16)
    grad_query_mat = contract_first(normed, grad_query_low)
    grad_key_mat = contract_first(normed, grad_key_low)
    grad_value_mat = contract_first(normed, grad_value_low)
    grad_normed = (
        contract_last(grad_query_low, query_mat)
        + contract_last(grad_key_low, key_mat)
        + contract_last(grad_value_low, value_mat)
    )
    grad_inputs_part, grad_first_gain = jax.vjp(rms_norm, inputs, first_gain)[1](grad_normed)
    input_grad = (grad_middle + grad_inputs_part).reshape(seq_count, block_len, D)
    count_dp = lax.axis_size("dp")
    count_seq = lax.axis_size("seq")
    owners = count_dp * count_seq
    owned = (
        lax.psum_scatter(
            grad_query_mat.reshape(owners, -1), ("dp", "seq"), scatter_dimension=0, tiled=True
        ),
        lax.psum_scatter(
            grad_key_mat.reshape(owners, -1), ("dp", "seq"), scatter_dimension=0, tiled=True
        ),
        lax.psum_scatter(
            grad_value_mat.reshape(owners, -1), ("dp", "seq"), scatter_dimension=0, tiled=True
        ),
        lax.psum_scatter(
            grad_out_mat.reshape(owners, -1), ("dp", "seq"), scatter_dimension=0, tiled=True
        ),
        lax.psum_scatter(
            grad_gate_mat.reshape(owners, -1), ("dp", "seq"), scatter_dimension=0, tiled=True
        ),
        lax.psum_scatter(
            grad_up_mat.reshape(owners, -1), ("dp", "seq"), scatter_dimension=0, tiled=True
        ),
        lax.psum_scatter(
            grad_down_mat.reshape(owners, -1), ("dp", "seq"), scatter_dimension=0, tiled=True
        ),
    )
    summed = tuple((piece.reshape(-1) for piece in owned))
    gain_total = jnp.concatenate([grad_first_gain, grad_second_gain])
    bias_total = jnp.concatenate(
        [
            jnp.sum(grad_query_low.astype(jnp.float32), axis=0),
            jnp.sum(grad_key_low.astype(jnp.float32), axis=0),
            jnp.sum(grad_value_low.astype(jnp.float32), axis=0),
        ]
    )
    gain_sum, bias_sum = lax.psum((gain_total, bias_total), ("dp", "seq"))
    seq_index = lax.axis_index("seq")
    gain_piece = gain_vector.shape[0]
    bias_piece = bias_vector.shape[0]
    gain_grad = lax.dynamic_slice_in_dim(gain_sum, seq_index * gain_piece, gain_piece)
    bias_grad = lax.dynamic_slice_in_dim(bias_sum, seq_index * bias_piece, bias_piece)
    return (
        output,
        input_grad,
        summed[0],
        summed[1],
        summed[2],
        summed[3],
        summed[4],
        summed[5],
        summed[6],
        gain_grad,
        bias_grad,
    )


def solution(mesh):
    in_specs = (
        P("dp", "seq", None),
        P("dp", "seq"),
        P(("dp", "seq")),
        P(("dp", "seq")),
        P(("dp", "seq")),
        P(("dp", "seq")),
        P(("dp", "seq")),
        P(("dp", "seq")),
        P(("dp", "seq")),
        P("seq"),
        P("seq"),
        P("dp", "seq", None),
    )
    out_specs = (
        P("dp", "seq", None),
        P("dp", "seq", None),
        P(("dp", "seq")),
        P(("dp", "seq")),
        P(("dp", "seq")),
        P(("dp", "seq")),
        P(("dp", "seq")),
        P(("dp", "seq")),
        P(("dp", "seq")),
        P("seq"),
        P("seq"),
    )
    return jax.shard_map(shards, mesh=mesh, in_specs=in_specs, out_specs=out_specs, check_vma=False)
```

profile of v0, /device:TPU:0, one launch (start us, length us, event | category | flops | bytes accessed | tf_op | source)
XLA Modules:
  0.0 1461.2 jit_solution(11780885291626035382)
XLA Ops:
  16.6 18.5 %all-reduce.11 = (bf16[1792]{0:T(1024)(128)(2,1)S(1)}, bf16[1152]{0:T(1024)(128)(2,1)S(1)}) all-reduce(bf16[1792]{0:T(1024)(128)(2,1)S(1)} %dynamic-update-slice, bf16[1152]{0:T(1024)(128)(2,1)S(1)} %dynamic-update-slice.1), channel_id=1, replica_groups=mesh['dp'=4,'seq'=8] {'seq'}, use_global_device_ids=true, to_apply=%add | all-reduce | flops 2944 | bytes 11776
  36.5 40.4 %all-gather.2 = bf16[32,1,3584]{2,1,0:T(2,128)(2,1)S(1)} all-gather(bf16[1,1,3584]{2,1,0:T(2,128)(2,1)S(1)} %reshape.375), channel_id=1, replica_groups=mesh['dp'=4,'seq'=8] {'dp','seq'}, dimensions={0}, use_global_device_ids=true | all-gather | bytes 236544 | tf_op jit(solution)/shard_map/all_gather | solution.py:156
  78.7 39.2 %all-gather.1 = bf16[32,1,3584]{2,1,0:T(2,128)(2,1)S(1)} all-gather(bf16[1,1,3584]{2,1,0:T(2,128)(2,1)S(1)} %reshape.373), channel_id=1, replica_groups=mesh['dp'=4,'seq'=8] {'dp','seq'}, dimensions={0}, use_global_device_ids=true | all-gather | bytes 236544 | tf_op jit(solution)/shard_map/all_gather | solution.py:155
  122.9 16.1 %all_gather.50 = bf16[2,1024,128]{2,1,0:T(8,128)(2,1)S(1)} all-gather(bf16[2,128,128]{2,1,0:T(8,128)(2,1)S(1)} %bitcast.276), channel_id=1, replica_groups=mesh['dp'=4,'seq'=8] {'seq'}, dimensions={1}, use_global_device_ids=true | all-gather | bytes 589824 | tf_op jit(solution)/shard_map/all_gather | solution.py:196
  140.3 16.1 %all_gather.48 = bf16[2,1024,128]{2,1,0:T(8,128)(2,1)S(1)} all-gather(bf16[2,128,128]{2,1,0:T(8,128)(2,1)S(1)} %bitcast.277), channel_id=1, replica_groups=mesh['dp'=4,'seq'=8] {'seq'}, dimensions={1}, use_global_device_ids=true | all-gather | bytes 589824 | tf_op jit(solution)/shard_map/all_gather | solution.py:195
  156.6 9.4 all_gather.43
  166.3 4.2 multiply_cosine_fusion
  174.0 10.8 reduce.4
  184.8 3.6 reshape.333
  188.4 12.0 reduce.7
  200.3 4.0 reshape.341
  204.4 3.0 convolution_add_fusion.3
  207.4 2.4 copy.63
  209.8 2.6 reshape.334
  213.8 1.8 fusion.65
  215.8 12.9 while.26
  217.2 2.0 fusion.155
  219.2 2.3 fusion.156
  223.6 2.0 fusion.155
  225.6 2.3 fusion.156
  228.7 1.6 copy.69
  232.2 16.4 %reshape.342 = bf16[896,4864]{1,0:T(8,128)(2,1)} reshape(bf16[4358144]{0:T(1024)(128)(2,1)} %all-gather.10.cloned.1.call-done) | data formatting | bytes 17432576 | tf_op jit(solution)/shard_map/reshape | solution.py:83
  248.6 49.2 %all-gather.12.cloned.1.call-done = bf16[4358144]{0:T(1024)(128)(2,1)} async-done(((bf16[136192]{0:T(1024)(128)(2,1)}), bf16[4358144]{0:T(1024)(128)(2,1)}) %all-gather.12.cloned.1.call-update) | async-done | bytes 8716304 | tf_op jit(solution)/shard_map/all_gather | solution.py:159
  297.8 16.4 %reshape.343 = bf16[896,4864]{1,0:T(8,128)(2,1)} reshape(bf16[4358144]{0:T(1024)(128)(2,1)} %all-gather.12.cloned.1.call-done) | data formatting | bytes 17432576 | tf_op jit(solution)/shard_map/reshape | solution.py:84
  314.2 8.0 fusion.95
  322.3 4.7 fusion.94
  326.9 51.2 %all-gather.14.cloned.1.call-done = bf16[4358144]{0:T(1024)(128)(2,1)} async-done(((bf16[136192]{0:T(1024)(128)(2,1)}), bf16[4358144]{0:T(1024)(128)(2,1)}) %all-gather.14.cloned.1.call-update) | async-done | bytes 8716304 | tf_op jit(solution)/shard_map/all_gather | solution.py:160
  378.1 16.4 %reshape.344 = bf16[4864,896]{1,0:T(8,128)(2,1)} reshape(bf16[4358144]{0:T(1024)(128)(2,1)} %all-gather.14.cloned.1.call-done) | data formatting | bytes 17432576 | tf_op jit(solution)/shard_map/reshape | solution.py:85
  394.6 10.0 multiply_convert_fusion.1
  404.6 2.8 fusion.96
  407.4 7.1 multiply_reduce_fusion.1
  416.4 2.3 fusion.77
  418.7 8.5 fusion.98
  429.4 46.8 %while.27 = (s32[]{:T(128)}, f32[2,2,7,128,64]{3,0,4,2,1:T(2,128)}, f32[2,2,1024,64]{2,3,1,0:T(8,128)}, bf16[2,2,1024,64]{2,3,1,0:T(8,128)(2,1)}, pred[2,128,102...) while((s32[]{:T(128)}, f32[2,2,7,128,64]{3,0,4,2,1:T(2,128)}, ...), condition=%wide.region_11.12_spmd, body=%wide.region_9.11_spmd.sunk | while | flops 1202174208 | bytes 68279496 | solution.py:248
  430.8 2.9 fusion.167
  433.7 2.6 multiply_reduce_fusion.5
  436.3 2.0 multiply_convert_fusion.5
  441.3 11.6 dynamic_update_slice.31
  454.1 2.9 fusion.167
  457.0 2.6 multiply_reduce_fusion.5
  459.6 2.0 multiply_convert_fusion.5
  464.6 11.6 dynamic_update_slice.31
  476.2 2.1 copy.76
  480.0 1.6 fusion.61
  482.6 3.5 reshape.356
  486.5 10.3 fusion.97
  497.2 2.2 convert_reduce_fusion
  499.5 2.3 fusion.73
  501.8 3.5 reshape.350
  505.3 22.8 %reshape.360 = f32[32,136192]{1,0:T(8,128)} reshape(f32[896,4864]{1,0:T(8,128)} %fusion.98) | data formatting | bytes 34865152 | tf_op jit(solution)/shard_map/reshape | solution.py:301
  528.1 22.8 %reshape.358 = f32[32,136192]{1,0:T(8,128)} reshape(f32[896,4864]{1,0:T(8,128)} %fusion.97) | data formatting | bytes 34865152 | tf_op jit(solution)/shard_map/reshape | solution.py:298
  550.9 8.5 fusion.99
  559.4 19.6 %reshape.362 = f32[32,136192]{1,0:T(8,128)} reshape(f32[4864,896]{1,0:T(8,128)} %fusion.99) | data formatting | bytes 34865152 | tf_op jit(solution)/shard_map/reshape | solution.py:304
  583.8 2.2 fusion.75
  586.0 9.3 fusion.56
  596.3 41.6 %all-reduce.9 = (f32[1792]{0:T(1024)S(1)}, f32[1152]{0:T(1024)S(1)}) all-reduce(f32[1792]{0:T(1024)S(1)} %pad_maximum_fusion.2, f32[1152]{0:T(1024)S(1)} %pad_maximum_fusion.3), channel_id=1, replica_groups=mesh['dp'=4,'seq'=8] {'dp','seq'}, use_global_device_ids=true, to_apply=%region_24.25 | all-reduce | flops 2944 | bytes 23552 | tf_op jit(solution)/shard_map/psum | solution.py:316
  640.4 797.1 %all-reduce.14.cloned.1.call-done = (f32[32,25088]{1,0:T(8,128)}, f32[32,3584]{1,0:T(8,128)}, f32[32,3584]{1,0:T(8,128)}, f32[32,25088]{1,0:T(8,128)}, f32[32,13...) async-done(((f32[32,25088]{1,0:T(8,128)}, f32[32,3584]{1,0:T(8,128)}, f32[32,3584]{1,0:T(8,128)}, f32[32,25088]{1,0:T(8,128)}, f32[32,136192]{1,0:T(8,128)}, ...) | async-done | bytes 59637776
  1437.5 2.1 dynamic-slice_reduce_fusion.1
  1439.5 1.5 dynamic-slice_reduce_fusion.3
  1441.1 1.5 dynamic-slice_reduce_fusion.2
  1442.6 2.1 dynamic-slice_reduce_fusion
  1444.7 3.2 constant_dynamic-slice_fusion.2
  1447.8 3.2 constant_dynamic-slice_fusion.1
  1451.0 3.2 constant_dynamic-slice_fusion
  (211 shorter events, 52.8 us)
Async XLA Ops:
  7.2 149.4 %copy-start.40 = (s32[2,128]{1,0:T(2,128)S(1)}, s32[2,128]{1,0:T(2,128)}, u32[]{:S(2)}) copy-start(s32[2,128]{1,0:T(2,128)} %param.17) | copy-start | bytes 3076
  7.2 166.8 %all-gather.16.cloned.1.call-start = ((), (), s32[]{:S(2)}) async-start(), calls=%async_computation.7 | async-start | bytes 3311616 | tf_op jit(solution)/shard_map/all_gather | solution.py:154
  8.8 179.6 %all-gather.18.cloned.1.call-start = ((), (), s32[]{:S(2)}) async-start(), calls=%async_computation.8 | async-start | bytes 3311616 | tf_op jit(solution)/shard_map/all_gather | solution.py:157
  10.3 221.9 %all-gather.10.cloned.1.call-start = ((), (), s32[]{:S(2)}) async-start(), calls=%async_computation.2 | async-start | bytes 8988672 | tf_op jit(solution)/shard_map/all_gather | solution.py:158
  11.1 286.7 %all-gather.12.cloned.1.call-start = ((), (), s32[]{:S(2)}) async-start(), calls=%async_computation.3 | async-start | bytes 8988672 | tf_op jit(solution)/shard_map/all_gather | solution.py:159
  11.6 366.5 %all-gather.14.cloned.1.call-start = ((), (), s32[]{:S(2)}) async-start(), calls=%async_computation.4 | async-start | bytes 8988672 | tf_op jit(solution)/shard_map/all_gather | solution.py:160
  12.2 566.8 %reduce-scatter.5.cloned.1.call-start = ((), (), s32[]{:S(2)}) async-start(), calls=%async_computation.6 | async-start | bytes 589824 | tf_op jit(solution)/shard_map/reduce_scatter | solution.py:265
  78.6 44.2 %copy-start.22 = (bf16[896,128]{1,0:T(8,128)(2,1)}, bf16[896,128]{1,0:T(8,128)(2,1)S(1)}, u32[]{:S(2)}) copy-start(bf16[896,128]{1,0:T(8,128)(2,1)S(1)} %reshape.338) | copy-start | bytes 688132
  119.5 20.8 %copy-start.24 = (bf16[896,128]{1,0:T(8,128)(2,1)}, bf16[896,128]{1,0:T(8,128)(2,1)S(1)}, u32[]{:S(2)}) copy-start(bf16[896,128]{1,0:T(8,128)(2,1)S(1)} %reshape.335) | copy-start | bytes 688132
  120.8 0.6 copy-start.38
  121.4 1.5 copy-start.36
  122.6 81.8 %copy-start.1 = (bf16[2,128,896]{2,1,0:T(8,128)(2,1)}, bf16[2,128,896]{2,1,0:T(8,128)(2,1)S(1)}, u32[]{:S(2)}) copy-start(bf16[2,128,896]{2,1,0:T(8,128)(2,1)S(1)} %fusion.69) | copy-start | bytes 1376260
  172.0 2.0 copy-start.14
  172.0 41.8 %copy-start.28 = (f32[2,128,64]{1,0,2:T(2,128)}, f32[2,128,64]{1,0,2:T(2,128)S(1)}, u32[]{:S(2)}) copy-start(f32[2,128,64]{1,0,2:T(2,128)S(1)} %get-tuple-element.236) | copy-start | bytes 196612
  172.1 41.8 %copy-start.32 = (f32[2,128,64]{1,0,2:T(2,128)}, f32[2,128,64]{1,0,2:T(2,128)S(1)}, u32[]{:S(2)}) copy-start(f32[2,128,64]{1,0,2:T(2,128)S(1)} %get-tuple-element.235) | copy-start | bytes 196612
  215.8 14.5 copy-start.5
  215.8 3.3 copy-start.12
  215.8 3.3 copy-start.34
  221.5 0.8 copy-start.35
  222.3 3.3 copy-start.12
  222.3 3.3 copy-start.34
  227.9 0.8 copy-start.35
  228.7 2.5 copy-start.7
  230.3 0.9 copy-start.17
  231.1 0.9 copy-start.9
  314.2 8.0 copy-start
  378.1 26.4 %slice-start = ((s8[8716288]{0:T(1024)(128)(4,1)}), s8[327680]{0:T(1024)(128)(4,1)S(1)}, s32[]{:S(2)}) async-start(s8[8716288]{0:T(1024)(128)(4,1)} %bitcast.247), calls=%async_computation.10 | async-start | bytes 655360
  394.6 10.0 slice-start.1
  394.6 10.0 slice-start.2
  404.6 2.8 copy-start.21
  404.6 2.8 copy-start.10
  407.4 7.2 copy-start.27
  407.4 9.0 copy-start.18
  414.9 1.5 copy-start.3
  418.7 8.5 copy-start.26
  418.7 10.7 copy-start.8
  418.7 10.7 copy-start.13
  436.3 3.3 copy-start.15
  440.4 1.0 copy-start.16
  459.6 3.3 copy-start.15
  463.7 1.0 copy-start.16
  476.2 5.4 copy-start.19
  476.2 5.4 copy-start.33
  478.4 102.7 %reduce-scatter.3.cloned.1.call-start = ((), (), s32[]{:S(2)}) async-start(), calls=%async_computation.5 | async-start | bytes 589824 | tf_op jit(solution)/shard_map/reduce_scatter | solution.py:262
  486.4 10.8 copy-start.29
  486.5 13.0 copy-start.2
  496.7 940.7 %all-reduce.14.cloned.1.call-start = ((), (), s32[]{:S(2)}) async-start(), calls=%async_computation.9 | async-start | bytes 119275520
  528.1 22.8 %copy-start.20 = (bf16[256,4864]{1,0:T(8,128)(2,1)S(1)}, bf16[256,4864]{1,0:T(8,128)(2,1)}, u32[]{:S(2)}) copy-start(bf16[256,4864]{1,0:T(8,128)(2,1)} %get-tuple-element.216) | copy-start | bytes 7471108
  583.0 0.7 copy-start.39
  583.0 2.9 copy-start.11
  586.0 9.4 copy-start.25
  586.0 9.3 copy-start.31
  586.0 9.6 copy-start.6
  586.0 9.6 copy-start.23
  586.0 9.6 copy-start.30
  586.0 9.6 copy-start.37
  586.0 10.1 copy-start.41
  586.0 53.1 %copy-start.4 = (f32[256,896]{1,0:T(8,128)S(1)}, f32[256,896]{1,0:T(8,128)}, u32[]{:S(2)}) copy-start(f32[256,896]{1,0:T(8,128)} %copy-done.3) | copy-start | bytes 2752516
Sparse Core Ops, SparseCore 0:
  11.4 62.4 all-gather.15
  77.3 59.5 all-gather.17
  139.8 77.6 all-gather.9
  220.3 77.4 all-gather.11
  300.6 77.4 all-gather.13
  478.5 29.5 reduce-scatter.4
  511.0 29.0 reduce-scatter.2
  583.2 854.2 all-reduce.13
where the time goes:
time: 1470 us; the launch traced here: 1460 us
  waiting for transfers between devices  899 us (61%)
  local copies, waits for them, and re-layouts  200 us (14%)
  blocking collectives  181 us (12%)
  matrix products  109 us (7%)
  other arithmetic  53.3 us (4%)
  between operations  16.5 us (1%)
    unnamed x9, waiting for transfers between devices  799 us
    all_gather x1, waiting for transfers between devices, shards(): lax.all_gather(w_down, ('dp', 'seq'), axis=0, tiled=True)  51.2 us
    all_gather x1, waiting for transfers between devices, shards(): lax.all_gather(w_up, ('dp', 'seq'), axis=0, tiled=True)  49.2 us
    psum x1, blocking collectives, shards(): gain_sum, bias_sum = lax.psum((gain_total, bias_total), ('dp', 'seq'))  41.6 us
    all_gather x1, blocking collectives, shards(): lax.all_gather(w_value, ('dp', 'seq'), axis=0, tiled=True)  40.4 us
    all_gather x1, blocking collectives, shards(): lax.all_gather(w_key, ('dp', 'seq'), axis=0, tiled=True)  39.2 us
    dot_general x7, matrix products, contract_first(): lax.dot_general(left, right, (((0,), (0,)), ((), ())), preferred_element_...  34.1 us
  transfers between devices with their start and end apart: 8, of which 3 were waited for; matrix products, arithmetic and copies ran while one was open for 16% of the time, Pallas kernels for 0%

commit v1 on v0

--- a/solution.py
+++ b/solution.py
@@ -129,7 +129,7 @@
     return (grad_queries, grad_keys, grad_values)
 
 
-def shards(
+def shards_flat(
     hidden_in,
     segments,
     w_query,
@@ -334,6 +334,222 @@
     )
 
 
+def spread(rows, block, spare):
+    place = jnp.arange(rows)
+    place = place // block * spare + place % block
+    width = rows // block * spare
+    return (place[:, None] == jnp.arange(width)[None, :]).astype(jnp.bfloat16)
+
+
+def round_up(value, step):
+    return -(-value // step) * step
+
+
+def shards_split(
+    hidden_in,
+    segments,
+    w_query,
+    w_key,
+    w_value,
+    w_out,
+    w_gate,
+    w_up,
+    w_down,
+    gain_vector,
+    bias_vector,
+    out_grad,
+):
+    low = jnp.bfloat16
+    seq_count, block_len, _ = hidden_in.shape
+    count_dp = lax.axis_size("dp")
+    count_seq = lax.axis_size("seq")
+    owners = count_dp * count_seq
+    dp_index = lax.axis_index("dp")
+    seq_index = lax.axis_index("seq")
+    seq_len = block_len * count_seq
+    offset = seq_index * block_len
+    row_count = seq_count * block_len
+    group_size = HEADS // KVH
+    own_rows = D // owners
+    block = round_up(own_rows + 1, 16)
+    own_units = FF // owners
+    unit_block = round_up(own_units, 16)
+    units = count_dp * unit_block
+    gain_piece = gain_vector.shape[0]
+    bias_piece = bias_vector.shape[0]
+    both = ("dp", "seq")
+
+    attn_width = 2 * D + 2 * KVW
+    attn_rows = jnp.concatenate(
+        [
+            w_query.reshape(own_rows, D),
+            w_key.reshape(own_rows, KVW),
+            w_value.reshape(own_rows, KVW),
+            w_out.reshape(own_rows, D),
+        ],
+        axis=1,
+    )
+    small = jnp.concatenate([gain_vector, bias_vector, segments.astype(low).reshape(-1)])
+    small = jnp.pad(small, (0, attn_width - small.shape[0]))[None]
+    attn_rows = jnp.concatenate(
+        [attn_rows, small, jnp.zeros((block - own_rows - 1, attn_width), low)], axis=0
+    )
+    attn_all = lax.all_gather(attn_rows, both, axis=0, tiled=True)
+    small_all = attn_all.reshape(owners, block, attn_width)[:, own_rows]
+    gain_full = small_all[:count_seq, :gain_piece].reshape(-1).astype(jnp.float32)
+    bias_wide = (
+        small_all[:count_seq, gain_piece : gain_piece + bias_piece].reshape(-1).astype(jnp.float32)
+    )
+    small_here = lax.dynamic_slice_in_dim(small_all, dp_index * count_seq, count_seq, 0)
+    doc_all = (
+        small_here[:, gain_piece + bias_piece : gain_piece + bias_piece + row_count]
+        .astype(jnp.int32)
+        .reshape(count_seq, seq_count, block_len)
+        .transpose(1, 0, 2)
+        .reshape(seq_count, seq_len)
+    )
+    first_gain = gain_full[:D]
+    second_gain = gain_full[D:]
+    pick = spread(D, own_rows, block)
+    attn_mat = matmul(pick, attn_all).astype(low)
+    qkv_mat = attn_mat[:, : D + 2 * KVW]
+    out_mat = attn_mat[:, D + 2 * KVW :]
+
+    def by_user(flat):
+        parts = flat.reshape(own_rows, count_dp, count_seq, own_units).transpose(2, 0, 1, 3)
+        parts = jnp.pad(
+            parts, ((0, 0), (0, block - own_rows), (0, 0), (0, unit_block - own_units))
+        )
+        return parts.reshape(count_seq, block, units)
+
+    gate_up_own = jnp.concatenate([by_user(w_gate), by_user(w_up)], axis=2)
+    gate_up_own = lax.all_to_all(gate_up_own, "seq", 0, 0, tiled=True)
+    gate_up_all = lax.all_gather(
+        gate_up_own.reshape(count_seq * block, 2 * units), "dp", axis=0, tiled=True
+    )
+    gate_up_mat = matmul(pick, gate_up_all).astype(low)
+    down_own = jnp.pad(w_down.reshape(own_units, D), ((0, unit_block - own_units), (0, 0)))
+    down_mat = lax.all_gather(down_own, "dp", axis=0, tiled=True)
+    grad_branch_all = lax.all_gather(out_grad.reshape(row_count, D), "seq", axis=0, tiled=True)
+
+    places_all = doc_places(doc_all)
+    cos_all, sin_all = rope_tables(places_all, HD)
+    cos_here = lax.dynamic_slice_in_dim(cos_all, offset, block_len, 1)
+    sin_here = lax.dynamic_slice_in_dim(sin_all, offset, block_len, 1)
+    key_index = jnp.arange(seq_len)
+    query_index = offset + jnp.arange(block_len)
+    allowed = (segments[:, :, None] == doc_all[:, None, :]) & (
+        key_index[None, None, :] <= query_index[None, :, None]
+    )
+    inputs = hidden_in.astype(jnp.float32).reshape(row_count, D)
+    normed = rms_norm(inputs, first_gain).astype(low)
+    qkv_pre = matmul(normed, qkv_mat) + bias_wide
+    query_pre = qkv_pre[:, :D]
+    key_value_low = qkv_pre[:, D:].astype(low).reshape(seq_count, block_len, 2 * KVW)
+    key_value_all = lax.all_gather(key_value_low, "seq", axis=1, tiled=True)
+    key_all = key_value_all[..., :KVW]
+    value_all = key_value_all[..., KVW:]
+    key_heads = (
+        key_all.astype(jnp.float32).reshape(seq_count, seq_len, KVH, HD).transpose(0, 2, 1, 3)
+    )
+    key_rot = turn(key_heads, cos_all[:, None], sin_all[:, None]).astype(low)
+    value_heads = value_all.reshape(seq_count, seq_len, KVH, HD).transpose(0, 2, 1, 3)
+    query_heads = query_pre.reshape(seq_count, block_len, KVH, group_size, HD).transpose(
+        0, 2, 3, 1, 4
+    )
+    query_rot = turn(query_heads, cos_here[:, None, None], sin_here[:, None, None]).astype(low)
+    mixed_heads, log_total = lax.map(attend_forward, (query_rot, key_rot, value_heads, allowed))
+    mixed_rows = mixed_heads.transpose(0, 3, 1, 2, 4).reshape(row_count, D).astype(low)
+    middle = inputs + matmul(mixed_rows, out_mat)
+    normed_two = rms_norm(middle, second_gain).astype(low)
+
+    normed_all = lax.all_gather(normed_two, "seq", axis=0, tiled=True)
+    gate_up_pre = matmul(normed_all, gate_up_mat)
+    gate_pre = gate_up_pre[:, :units]
+    up_pre = gate_up_pre[:, units:]
+    activated = gated(gate_pre, up_pre).astype(low)
+    grad_act = contract_last(grad_branch_all, down_mat)
+    grad_gate_pre, grad_up_pre = jax.vjp(gated, gate_pre, up_pre)[1](grad_act)
+    grad_gate_up = jnp.concatenate([grad_gate_pre.astype(low), grad_up_pre.astype(low)], axis=1)
+    grad_normed_part = contract_last(grad_gate_up, gate_up_mat).astype(low)
+    grad_normed_two = lax.psum_scatter(
+        grad_normed_part, "seq", scatter_dimension=0, tiled=True
+    ).astype(jnp.float32)
+    branch_part = matmul(activated, down_mat).astype(low)
+    branch = lax.psum_scatter(branch_part, "seq", scatter_dimension=0, tiled=True)
+    output = (middle + branch.astype(jnp.float32)).astype(low).reshape(seq_count, block_len, D)
+
+    grad_gate_up_mat = contract_first(normed_all, grad_gate_up).astype(low)
+    grad_gate_up_mat = contract_first(pick, grad_gate_up_mat).astype(low)
+    grad_down_mat = contract_first(activated, grad_branch_all).astype(low)
+    grad_gate_up_sum = lax.psum_scatter(grad_gate_up_mat, "dp", scatter_dimension=0, tiled=True)
+    grad_down_sum = lax.psum_scatter(grad_down_mat, "dp", scatter_dimension=0, tiled=True)
+    grad_down = grad_down_sum[:own_units].astype(jnp.float32).reshape(-1)
+    grad_gate_up_own = lax.all_to_all(
+        grad_gate_up_sum.reshape(count_seq, block, 2 * units), "seq", 0, 0, tiled=True
+    )
+    grad_gate_up_own = (
+        grad_gate_up_own[:, :own_rows]
+        .reshape(count_seq, own_rows, 2, count_dp, unit_block)[..., :own_units]
+        .transpose(2, 1, 3, 0, 4)
+        .reshape(2, -1)
+        .astype(jnp.float32)
+    )
+
+    grad_result = out_grad.astype(jnp.float32).reshape(row_count, D)
+    grad_middle_part, grad_second_gain = jax.vjp(rms_norm, middle, second_gain)[1](grad_normed_two)
+    grad_middle = grad_result + grad_middle_part
+    grad_attn = grad_middle.astype(low)
+    pick_rows = lambda values: matmul(values, pick).astype(low)
+    grad_out_mat = contract_first(pick_rows(mixed_rows), grad_attn).astype(low)
+    grad_out_sum = lax.psum_scatter(grad_out_mat, both, scatter_dimension=0, tiled=True)
+    grad_mixed = contract_last(grad_attn, out_mat).astype(low)
+    grad_mixed = grad_mixed.reshape(seq_count, block_len, KVH, group_size, HD).transpose(
+        0, 2, 3, 1, 4
+    )
+    grad_query_rot, grad_key_rot, grad_value_heads = lax.map(
+        attend_backward, (query_rot, key_rot, value_heads, allowed, log_total, grad_mixed)
+    )
+    grad_query_pre = unturn(grad_query_rot, cos_here[:, None, None], sin_here[:, None, None])
+    grad_query_low = grad_query_pre.transpose(0, 3, 1, 2, 4).reshape(row_count, D).astype(low)
+    grad_key_all = (
+        unturn(grad_key_rot, cos_all[:, None], sin_all[:, None])
+        .transpose(0, 2, 1, 3)
+        .reshape(seq_count, seq_len, KVW)
+    )
+    grad_value_all = grad_value_heads.transpose(0, 2, 1, 3).reshape(seq_count, seq_len, KVW)
+    grad_key_value = jnp.concatenate([grad_key_all, grad_value_all], axis=-1).astype(low)
+    grad_key_value_low = lax.psum_scatter(
+        grad_key_value, "seq", scatter_dimension=1, tiled=True
+    ).reshape(row_count, 2 * KVW)
+    grad_qkv_low = jnp.concatenate([grad_query_low, grad_key_value_low], axis=1)
+    grad_qkv_mat = contract_first(pick_rows(normed), grad_qkv_low)
+    grad_normed = contract_last(grad_qkv_low, qkv_mat)
+    grad_inputs_part, grad_first_gain = jax.vjp(rms_norm, inputs, first_gain)[1](grad_normed)
+    input_grad = (grad_middle + grad_inputs_part).reshape(seq_count, block_len, D)
+    gain_total = jnp.concatenate([grad_first_gain, grad_second_gain]).reshape(count_seq, gain_piece)
+    bias_total = jnp.sum(grad_qkv_low.astype(jnp.float32), axis=0).reshape(count_seq, bias_piece)
+    gain_sum, bias_sum = lax.psum((gain_total, bias_total), both)
+    gain_grad = lax.dynamic_slice_in_dim(gain_sum, seq_index, 1, 0).reshape(-1)
+    bias_grad = lax.dynamic_slice_in_dim(bias_sum, seq_index, 1, 0).reshape(-1)
+    grad_qkv_sum = lax.psum_scatter(
+        grad_qkv_mat.astype(low), both, scatter_dimension=0, tiled=True
+    )[:own_rows].astype(jnp.float32)
+    return (
+        output,
+        input_grad,
+        grad_qkv_sum[:, :D].reshape(-1),
+        grad_qkv_sum[:, D : D + KVW].reshape(-1),
+        grad_qkv_sum[:, D + KVW :].reshape(-1),
+        grad_out_sum[:own_rows].astype(jnp.float32).reshape(-1),
+        grad_gate_up_own[0],
+        grad_gate_up_own[1],
+        grad_down,
+        gain_grad,
+        bias_grad,
+    )
+
+
 def solution(mesh):
     in_specs = (
         P("dp", "seq", None),
@@ -362,4 +578,7 @@
         P("seq"),
         P("seq"),
     )
+    owners = mesh.size
+    whole_rows = D % owners == 0 and FF % owners == 0
+    shards = shards_split if whole_rows else shards_flat
     return jax.shard_map(shards, mesh=mesh, in_specs=in_specs, out_specs=out_specs, check_vma=False)

time: 1470 us -> 768 us (0.52)
  waiting for transfers between devices: 899 us -> 490 us
  blocking collectives: 181 us -> 39.7 us
  local copies, waits for them, and re-layouts: 200 us -> 60.8 us
  other arithmetic: 53.3 us -> 36.8 us
    unnamed x9 -> x14, waiting for transfers between devices: 799 us -> 19.5 us
    reduce_scatter x2 -> x6, waiting for transfers between devices: 0.01 us -> 278 us  [the longest x1 100 us: shards_split(): lax.psum_scatter(grad_qkv_mat.astype(low), both, scatter_dimension=0, til...]
    reshape x20 -> x16, local copies, waits for them, and re-layouts: 142 us -> 9.92 us  [the longest x2 2.68 us: by_user(): flat.reshape(own_rows, count_dp, count_seq, own_units).transpose(2, 0, 1, 3)]
    all_gather x5 -> x0, blocking collectives: 121 us -> none  [the longest x1 40.4 us: shards(): lax.all_gather(w_value, ('dp', 'seq'), axis=0, tiled=True)]
    all_gather x5 -> x6, waiting for transfers between devices: 100 us -> 169 us  [the longest x1 63.1 us: shards_split(): attn_all = lax.all_gather(attn_rows, both, axis=0, tiled=True)]
    all_gather x4 -> x0, other arithmetic: 25.5 us -> none  [the longest x1 12 us: shards(): lax.all_gather(w_out, ('dp', 'seq'), axis=0, tiled=True)]
    all_to_all x0 -> x2, waiting for transfers between devices: none -> 23.7 us  [the longest x1 23.7 us: shards_split(): gate_up_own = lax.all_to_all(gate_up_own, 'seq', 0, 0, tiled=True)]
    unnamed x1 -> x0, blocking collectives: 18.5 us -> none
  transfers between devices with their start and end apart: 8 -> 15, of which waited for: 3 -> 12; matrix products, arithmetic and copies ran while one was open for 16% -> 21% of each run, Pallas kernels for 0% -> 0%
where the time goes in v1:
time: 768 us; the launch traced here: 760 us
  waiting for transfers between devices  490 us (64%)
  matrix products  108 us (14%)
  local copies, waits for them, and re-layouts  60.8 us (8%)
  blocking collectives  39.7 us (5%)
  other arithmetic  36.8 us (5%)
  between operations  15.3 us (2%)
  starting transfers between devices  8.88 us (1%)
    reduce_scatter x1, waiting for transfers between devices, shards_split(): lax.psum_scatter(grad_qkv_mat.astype(low), both, scatter_dimension=0, til...  100 us
    reduce_scatter x1, waiting for transfers between devices, shards_split(): lax.psum_scatter(grad_out_mat, both, scatter_dimension=0, tiled=True)  85.8 us
    all_gather x1, waiting for transfers between devices, shards_split(): attn_all = lax.all_gather(attn_rows, both, axis=0, tiled=True)  63.1 us
    reduce_scatter x1, waiting for transfers between devices, shards_split(): lax.psum_scatter(branch_part, 'seq', scatter_dimension=0, tiled=True)  44.4 us
    all_gather x1, waiting for transfers between devices, shards_split(): lax.all_gather(out_grad.reshape(row_count, D), 'seq', axis=0, tiled=True)  44.1 us
    psum x1, blocking collectives, shards_split(): gain_sum, bias_sum = lax.psum((gain_total, bias_total), both)  39.7 us
    all_gather x1, waiting for transfers between devices, shards_split(): normed_all = lax.all_gather(normed_two, 'seq', axis=0, tiled=True)  38.9 us
    dot_general x6, matrix products, matmul(): return jnp.dot(left, right, preferred_element_type=jnp.float32)  33.3 us
  transfers between devices with their start and end apart: 15, of which 12 were waited for; matrix products, arithmetic and copies ran while one was open for 21% of the time, Pallas kernels for 0%

profile of v1, /device:TPU:0, one launch (start us, length us, event | category | flops | bytes accessed | tf_op | source)
XLA Modules:
  0.0 760.0 jit_solution(7175520511273263422)
XLA Ops:
  10.5 1.5 maximum_maximum_fusion
  13.8 63.1 %all-gather.7.cloned.1.call-done = bf16[1024,2048]{1,0:T(8,128)(2,1)} async-done(((bf16[32,2048]{1,0:T(8,128)(2,1)}), bf16[1024,2048]{1,0:T(8,128)(2,1)}) %all-gather.7.cloned.1.call-update) | async-done | bytes 4194320 | tf_op jit(solution)/shard_map/all_gather | solution.py:397
  77.0 1.5 slice.139
  78.8 1.2 multiply_convert_fusion.3
  80.1 6.7 fusion.61
  89.3 1.3 reshape.324
  91.4 1.3 reshape.326
  94.4 3.5 all-to-all-start
  98.2 23.7 %all-to-all-done = bf16[8,32,1280]{2,1,0:T(8,128)(2,1)S(1)} async-done(((bf16[8,32,1280]{2,1,0:T(8,128)(2,1)}), bf16[8,32,1280]{2,1,0:T(8,128)(2,1)S(1)}, u32[]{:S(2)}, u32[]{:S(2)}) %all-to-all-start) | async-done | bytes 655392 | tf_op jit(solution)/shard_map/all_to_all | solution.py:426
  123.9 4.0 multiply_cosine_fusion
  131.3 2.3 fusion.128
  133.8 1.6 copy.85
  135.5 1.4 fusion.86
  136.9 12.9 %while.26 = (s32[]{:T(128)}, bf16[2,2,7,128,64]{3,4,2,1,0:T(8,128)(2,1)}, f32[2,2,7,128]{3,2,1,0:T(8,128)S(1)}, pred[2,128,1024]{2,1,0:T(8,128)(4,1)S(1)}, bf16[...) while((s32[]{:T(128)}, ...), condition=%wide.region_6.7_spmd, body=%wide.region_3.6_spmd.sunk | while | flops 491780352 | bytes 27622556 | solution.py:461
  136.9 1.4 fusion.164
  138.3 2.0 fusion.165
  140.2 2.3 fusion.166
  143.3 1.4 fusion.164
  144.7 2.0 fusion.165
  146.7 2.3 fusion.166
  149.7 1.5 copy.90
  151.3 2.4 multiply_reduce_fusion.2
  156.8 4.3 all-gather.13.cloned.1.call-done
  161.1 5.8 fusion.62
  167.0 38.9 %all-gather.11.cloned.1.call-done = bf16[2048,896]{1,0:T(8,128)(2,1)} async-done(((bf16[256,896]{1,0:T(8,128)(2,1)}), bf16[2048,896]{1,0:T(8,128)(2,1)}) %all-gather.11.cloned.1.call-update) | async-done | bytes 3670032 | tf_op jit(solution)/shard_map/all_gather | solution.py:466
  205.8 10.4 %fusion.131 = f32[2048,1280]{0,1:T(8,128)} fusion(bf16[2048,896]{1,0:T(8,128)(2,1)} %all-gather.11.cloned.1.call-done, bf16[896,1280]{1,0:T(8,128)(2,1)} %fusion.62), kind=kOutput, calls=%fused_computation.224 | convolution fusion | flops 4697620480 | bytes 16449536 | tf_op jit(solution)/shard_map/dot_general | solution.py:62
  216.2 18.2 %all-gather.15.cloned.1.call-done = bf16[640,896]{1,0:T(8,128)(2,1)} async-done(((bf16[160,896]{1,0:T(8,128)(2,1)}), bf16[640,896]{1,0:T(8,128)(2,1)}) %all-gather.15.cloned.1.call-update) | async-done | bytes 1146896 | tf_op jit(solution)/shard_map/all_gather | solution.py:432
  234.5 44.1 %all-gather.17.cloned.1.call-done = bf16[2048,896]{1,0:T(8,128)(2,1)} async-done(((bf16[256,896]{1,0:T(8,128)(2,1)}), bf16[2048,896]{1,0:T(8,128)(2,1)}) %all-gather.17.cloned.1.call-update) | async-done | bytes 3670032 | tf_op jit(solution)/shard_map/all_gather | solution.py:433
  278.6 10.3 %fusion.54 = (bf16[2048,640]{0,1:T(8,128)(2,1)S(1)}, bf16[2048,640]{0,1:T(8,128)(2,1)S(1)}, bf16[2048,640]{0,1:T(8,128)(2,1)}) fusion(f32[2048,1280]{0,1:T(8,128)} %fusion.131, bf16[640,896]{1,0:T(8,128)(2,1)} %all-gather.15.cloned.1.call-done, bf16[2048,896]{1,0:T(8,128)(2,1)} %all-gather.17.cloned.1.call-done), kind=kOutput, calls=%fused_computation.62 | convolution fusion | flops 2369781760 | bytes 23166976 | tf_op jit(solution)/shard_map/dot_general | solution.py:66
  288.9 1.5 copy-done.37
  291.2 7.1 convolution_convert_fusion.3
  298.6 7.2 convolution_convert_fusion.4
  305.9 14.1 %convolution_convert_fusion = bf16[1024,1280]{1,0:T(8,128)(2,1)} fusion(s32[896]{0:T(1024)S(1)} %fusion.116, bf16[2048,896]{1,0:T(8,128)(2,1)} %all-gather.11.cloned.1.call-done, bf16[2048,640]{0,1:T(8,128)(2,1)} %copy-done.38, bf16[2048,640]{0,1:T(8,128)(2,1)} %copy-done.37), kind=kOutput, calls=%fused_computation.70 | convolution fusion | flops 7060291584 | bytes 11537920 | tf_op jit(solution)/shard_map/dot_general | solution.py:72
  320.3 22.1 %reduce-scatter.12.cloned.1.call-done = bf16[256,896]{1,0:T(8,128)(2,1)} async-done(((bf16[2048,896]{1,0:T(8,128)(2,1)}), bf16[256,896]{1,0:T(8,128)(2,1)}) %reduce-scatter.12.cloned.1.call-update) | async-done | bytes 458768 | tf_op jit(solution)/shard_map/reduce_scatter | solution.py:475
  342.4 1.3 fusion.89
  343.7 44.4 %reduce-scatter.10.cloned.1.call-done = bf16[256,896]{1,0:T(8,128)(2,1)} async-done(((bf16[2048,896]{1,0:T(8,128)(2,1)}), bf16[256,896]{1,0:T(8,128)(2,1)}) %reduce-scatter.10.cloned.1.call-update) | async-done | bytes 458768 | tf_op jit(solution)/shard_map/reduce_scatter | solution.py:479
  388.2 2.3 fusion.90
  391.3 2.2 fusion.80
  394.0 46.7 %while.27 = (s32[]{:T(128)}, f32[2,2,7,128,64]{3,0,4,2,1:T(2,128)}, f32[2,2,1024,64]{2,3,1,0:T(8,128)}, bf16[2,2,1024,64]{2,3,1,0:T(8,128)(2,1)}, pred[2,128,102...) while((s32[]{:T(128)}, f32[2,2,7,128,64]{3,0,4,2,1:T(2,128)}, ...), condition=%wide.region_13.14_spmd, body=%wide.region_11.13_spmd.sunk | while | flops 1202174208 | bytes 68279496 | solution.py:510
  395.2 2.8 fusion.177
  398.0 2.6 multiply_reduce_fusion.5
  400.6 2.0 multiply_convert_fusion.5
  402.7 1.2 convolution_multiply_fusion.2
  405.8 11.6 %dynamic_update_slice.31 = f32[2,2,7,128,64]{3,0,4,2,1:T(2,128)} dynamic-update-slice(f32[2,2,7,128,64]{3,0,4,2,1:T(2,128)} %get-tuple-element.399, f32[1,2,7,128,64]{3,0,4,2,1:T(1,128)S(1)} %bitcast.263, s32[]{:T(128)S(6)} %copy.166, s32[]{:T(128)} %constant.95.clone.1..sunk, s32[]{:T(128)} %constant.95.clone.1..sunk, s32[]{:T(128)} %constant.95.clone.1..sunk, s32[]{:T(128)} %constant.95.clone.1..sunk) | dynamic-update-slice | bytes 917508 | tf_op jit(solution)/shard_map/while/body/jit(dynamic_update_index_in_dim)/dynamic_update_slice | solution.py:461
  418.5 2.9 fusion.177
  421.4 2.6 multiply_reduce_fusion.5
  424.0 2.0 multiply_convert_fusion.5
  426.1 1.2 convolution_multiply_fusion.2
  429.1 11.6 %dynamic_update_slice.31 = f32[2,2,7,128,64]{3,0,4,2,1:T(2,128)} dynamic-update-slice(f32[2,2,7,128,64]{3,0,4,2,1:T(2,128)} %get-tuple-element.399, f32[1,2,7,128,64]{3,0,4,2,1:T(1,128)S(1)} %bitcast.263, s32[]{:T(128)S(6)} %copy.166, s32[]{:T(128)} %constant.95.clone.1..sunk, s32[]{:T(128)} %constant.95.clone.1..sunk, s32[]{:T(128)} %constant.95.clone.1..sunk, s32[]{:T(128)} %constant.95.clone.1..sunk) | dynamic-update-slice | bytes 917508 | tf_op jit(solution)/shard_map/while/body/jit(dynamic_update_index_in_dim)/dynamic_update_slice | solution.py:461
  440.7 1.4 broadcast_multiply_fusion
  444.7 1.2 copy.128
  446.0 6.8 convolution_convert_fusion.6
  453.2 2.9 convolution_convert_fusion.5
  456.2 3.6 all-to-all-start.1
  460.8 18.8 %reduce-scatter.22.cloned.1.call-done = bf16[128,512]{1,0:T(8,128)(2,1)} async-done(((bf16[1024,512]{1,0:T(8,128)(2,1)}), bf16[128,512]{1,0:T(8,128)(2,1)}) %reduce-scatter.22.cloned.1.call-update) | async-done | bytes 131088
  480.7 4.3 convolution_convert_fusion.1
  485.0 25.4 %reduce-scatter.20.cloned.1.call-done = bf16[160,896]{1,0:T(8,128)(2,1)} async-done(((bf16[640,896]{1,0:T(8,128)(2,1)}), bf16[160,896]{1,0:T(8,128)(2,1)}) %reduce-scatter.20.cloned.1.call-update) | async-done | bytes 286736 | tf_op jit(solution)/shard_map/reduce_scatter | solution.py:486
  514.5 1.7 squeeze.44
  516.3 1.7 squeeze.43
  518.1 2.8 multiply_reduce_fusion.1
  521.3 39.7 %all-reduce.4 = (f32[8,224]{1,0:T(8,128)S(1)}, f32[8,144]{1,0:T(8,128)S(1)}) all-reduce(f32[8,224]{1,0:T(8,128)S(1)} %pad_maximum_fusion.12, f32[8,144]{1,0:T(8,128)S(1)} %reshape.348), channel_id=1, replica_groups=mesh['dp'=4,'seq'=8] {'dp','seq'}, use_global_device_ids=true, to_apply=%region_22.23 | all-reduce | flops 2944 | bytes 23552 | tf_op jit(solution)/shard_map/psum | solution.py:532
  562.2 1.2 fusion.91
  563.4 85.8 %reduce-scatter.16.cloned.1.call-done = bf16[32,896]{1,0:T(8,128)(2,1)} async-done(((bf16[1024,896]{1,0:T(8,128)(2,1)}), bf16[32,896]{1,0:T(8,128)(2,1)}) %reduce-scatter.16.cloned.1.call-update) | async-done | bytes 57360 | tf_op jit(solution)/shard_map/reduce_scatter | solution.py:505
  650.6 100.2 %reduce-scatter.14.cloned.1.call-done = bf16[32,1152]{1,0:T(8,128)(2,1)} async-done(((bf16[1024,1152]{1,0:T(8,128)(2,1)}), bf16[32,1152]{1,0:T(8,128)(2,1)}) %reduce-scatter.14.cloned.1.call-update) | async-done | bytes 73744 | tf_op jit(solution)/shard_map/reduce_scatter | solution.py:535
  (222 shorter events, 43.8 us)
Async XLA Ops:
  7.2 69.8 %all-gather.7.cloned.1.call-start = ((), (), s32[]{:S(2)}) async-start(), calls=%async_computation.9 | async-start | bytes 4325376 | tf_op jit(solution)/shard_map/all_gather | solution.py:397
  12.0 119.3 %all-gather.9.cloned.1.call-start = ((), (), s32[]{:S(2)}) async-start(), calls=%async_computation.10 | async-start | bytes 1179648 | tf_op jit(solution)/shard_map/all_gather | solution.py:449
  13.3 0.6 copy-start.30
  13.8 66.2 %copy-start.32 = (f32[256]{0:T(256)}, f32[256]{0:T(256)S(1)}, u32[]{:S(2)}) copy-start(f32[256]{0:T(256)S(1)} %bitcast_rsqrt_fusion) | copy-start | bytes 3076
  78.8 1.2 copy-start.28
  80.0 6.7 copy-start.24
  86.8 1.8 copy-start.35
  86.8 2.5 copy-start.26
  86.8 4.6 copy-start.27
  88.5 34.5 %copy-start.8 = (f32[256,1152]{1,0:T(8,128)}, f32[256,1152]{1,0:T(8,128)S(1)}, u32[]{:S(2)}) copy-start(f32[256,1152]{1,0:T(8,128)S(1)} %convolution_add_fusion) | copy-start | bytes 3538948
  92.9 30.7 %copy-start.34 = (s32[2,128]{1,0:T(2,128)S(1)}, s32[2,128]{1,0:T(2,128)}, u32[]{:S(2)}) copy-start(s32[2,128]{1,0:T(2,128)} %param.17) | copy-start | bytes 3076
  94.4 27.5 %all-to-all-start = ((bf16[8,32,1280]{2,1,0:T(8,128)(2,1)}), bf16[8,32,1280]{2,1,0:T(8,128)(2,1)S(1)}, u32[]{:S(2)}, u32[]{:S(2)}) async-start(bf16[8,32,1280]{2,1,0:T(8,128)(2,1)} %pad_maximum_fusion.4), calls=%async_computation | async-start | bytes 1310720 | tf_op jit(solution)/shard_map/all_to_all | solution.py:426
  97.9 63.2 %all-gather.13.cloned.1.call-start = ((), (), s32[]{:S(2)}) async-start(), calls=%async_computation.12 | async-start | bytes 3276800 | tf_op jit(solution)/shard_map/all_gather | solution.py:427
  121.9 0.8 copy-start.12
  122.8 83.1 %all-gather.11.cloned.1.call-start = ((), (), s32[]{:S(2)}) async-start(), calls=%async_computation.11 | async-start | bytes 4128768 | tf_op jit(solution)/shard_map/all_gather | solution.py:466
  123.0 6.4 slice-start
  128.3 2.2 copy-start.16
  128.3 2.2 copy-start.18
  129.4 6.0 copy-start
  136.9 14.4 %copy-start.6 = (bf16[2,128,896]{2,1,0:T(8,128)(2,1)S(1)}, bf16[2,128,896]{2,1,0:T(8,128)(2,1)}, u32[]{:S(2)}) copy-start(bf16[2,128,896]{2,1,0:T(8,128)(2,1)} %param.16) | copy-start | bytes 1376260
  138.3 2.0 copy-start.22
  142.5 0.8 copy-start.23
  144.7 2.0 copy-start.22
  149.0 0.8 copy-start.23
  149.7 5.0 copy-start.25
  151.3 2.4 copy-start.20
  154.7 79.8 %all-gather.15.cloned.1.call-start = ((), (), s32[]{:S(2)}) async-start(), calls=%async_computation.13 | async-start | bytes 1433600 | tf_op jit(solution)/shard_map/all_gather | solution.py:432
  155.8 122.8 %all-gather.17.cloned.1.call-start = ((), (), s32[]{:S(2)}) async-start(), calls=%async_computation.15 | async-start | bytes 4128768 | tf_op jit(solution)/shard_map/all_gather | solution.py:433
  156.4 186.0 %reduce-scatter.12.cloned.1.call-start = ((), (), s32[]{:S(2)}) async-start(), calls=%async_computation.16 | async-start | bytes 4128768 | tf_op jit(solution)/shard_map/reduce_scatter | solution.py:475
  278.6 12.6 %copy-start.36 = (bf16[896,1280]{1,0:T(8,128)(2,1)S(1)}, bf16[896,1280]{1,0:T(8,128)(2,1)}, u32[]{:S(2)}) copy-start(bf16[896,1280]{1,0:T(8,128)(2,1)} %fusion.62) | copy-start | bytes 6881284
  288.9 1.5 copy-start.37
  288.9 2.3 copy-start.38
  298.3 89.8 %reduce-scatter.10.cloned.1.call-start = ((), (), s32[]{:S(2)}) async-start(), calls=%async_computation.14 | async-start | bytes 4128768 | tf_op jit(solution)/shard_map/reduce_scatter | solution.py:479
  305.8 150.4 %reduce-scatter.18.cloned.1.call-start = ((), (), s32[]{:S(2)}) async-start(), calls=%async_computation.19 | async-start | bytes 3276800 | tf_op jit(solution)/shard_map/reduce_scatter | solution.py:485
  320.0 68.1 %copy-start.15 = (bf16[2,128,896]{2,1,0:T(8,128)(2,1)S(1)}, bf16[2,128,896]{2,1,0:T(8,128)(2,1)}, u32[]{:S(2)}) copy-start(bf16[2,128,896]{2,1,0:T(8,128)(2,1)} %param.27) | copy-start | bytes 1376260
  320.0 159.6 %reduce-scatter.22.cloned.1.call-start = ((), (), s32[]{:S(2)}) async-start(), calls=%async_computation.21 | async-start | bytes 1179648
  390.4 0.9 copy-start.10
  393.9 46.7 %copy-start.1 = (f32[2,1024,64]{1,2,0:T(8,128)S(1)}, f32[2,1024,64]{1,2,0:T(8,128)}, u32[]{:S(2)}) copy-start(f32[2,1024,64]{1,2,0:T(8,128)} %copy-done) | copy-start | bytes 1572868
  402.7 1.3 copy-start.3
  404.8 1.0 copy-start.4
  426.0 1.3 copy-start.3
  428.1 1.0 copy-start.4
  440.7 1.6 copy-start.2
  440.7 1.7 copy-start.5
  445.9 7.2 copy-start.11
  445.9 7.2 copy-start.21
  445.9 64.5 %reduce-scatter.20.cloned.1.call-start = ((), (), s32[]{:S(2)}) async-start(), calls=%async_computation.20 | async-start | bytes 1433600 | tf_op jit(solution)/shard_map/reduce_scatter | solution.py:486
  452.8 7.0 copy-start.9
  452.8 7.0 copy-start.19
  452.8 196.3 %reduce-scatter.16.cloned.1.call-start = ((), (), s32[]{:S(2)}) async-start(), calls=%async_computation.18 | async-start | bytes 1892352 | tf_op jit(solution)/shard_map/reduce_scatter | solution.py:505
  456.1 4.0 copy-start.17
  456.2 56.1 %all-to-all-start.1 = ((bf16[8,32,1280]{2,1,0:T(8,128)(2,1)}), bf16[8,32,1280]{2,1,0:T(8,128)(2,1)S(1)}, u32[]{:S(2)}, u32[]{:S(2)}) async-start(bf16[8,32,1280]{2,1,0:T(8,128)(2,1)} %bitcast.285), calls=%async_computation.6 | async-start | bytes 1310720 | tf_op jit(solution)/shard_map/all_to_all | solution.py:488
  459.7 291.1 %reduce-scatter.14.cloned.1.call-start = ((), (), s32[]{:S(2)}) async-start(), calls=%async_computation.17 | async-start | bytes 2433024 | tf_op jit(solution)/shard_map/reduce_scatter | solution.py:535
  460.8 24.2 %copy-start.13 = (bf16[112,8,2,128]{3,1,2,0:T(8,128)(2,1)}, bf16[112,8,2,128]{3,1,2,0:T(8,128)(2,1)S(1)}, u32[]{:S(2)}) copy-start(bf16[112,8,2,128]{3,1,2,0:T(8,128)(2,1)S(1)} %copy.144) | copy-start | bytes 1376260
  514.2 3.9 copy-start.7
  514.3 3.8 copy-start.29
  514.3 3.8 copy-start.33
  516.3 4.6 copy-start.14
  518.0 44.1 %copy-start.31 = (f32[2,128]{1,0:T(2,128)S(1)}, f32[2,128]{1,0:T(2,128)}, u32[]{:S(2)}) copy-start(f32[2,128]{1,0:T(2,128)} %copy-done.30) | copy-start | bytes 3076
Sparse Core Ops, SparseCore 0:
  12.1 64.8 all-gather.6
  89.4 25.6 all-gather.8
  122.9 38.2 all-gather.12
  163.2 42.5 all-gather.10
  208.1 26.3 all-gather.14
  235.9 42.5 all-gather.16
  298.4 43.9 reduce-scatter.11
  344.7 43.4 reduce-scatter.9
  391.1 37.9 reduce-scatter.17
  446.0 33.5 reduce-scatter.21
  482.5 27.8 reduce-scatter.19
  512.5 136.5 reduce-scatter.15
  655.3 95.4 reduce-scatter.13

commit v2 on v1

--- a/solution.py
+++ b/solution.py
@@ -395,6 +395,25 @@
         [attn_rows, small, jnp.zeros((block - own_rows - 1, attn_width), low)], axis=0
     )
     attn_all = lax.all_gather(attn_rows, both, axis=0, tiled=True)
+    pick = spread(D, own_rows, block)
+
+    def to_all_dp(piece):
+        copies = jnp.broadcast_to(piece[None], (count_dp, *piece.shape))
+        return lax.all_to_all(copies, "dp", 0, 0, tiled=True).reshape(-1, piece.shape[1])
+
+    def by_user(flat):
+        parts = flat.reshape(own_rows, count_dp, count_seq, own_units).transpose(2, 0, 1, 3)
+        parts = jnp.pad(
+            parts, ((0, 0), (0, block - own_rows), (0, 0), (0, unit_block - own_units))
+        )
+        return parts.reshape(count_seq, block, units)
+
+    gate_up_own = jnp.concatenate([by_user(w_gate), by_user(w_up)], axis=2)
+    gate_up_own = lax.all_to_all(gate_up_own, "seq", 0, 0, tiled=True)
+    gate_up_all = to_all_dp(gate_up_own.reshape(count_seq * block, 2 * units))
+    down_own = jnp.pad(w_down.reshape(own_units, D), ((0, unit_block - own_units), (0, 0)))
+    down_mat = to_all_dp(down_own)
+    attn_all, gate_up_all, down_mat = lax.optimization_barrier((attn_all, gate_up_all, down_mat))
     small_all = attn_all.reshape(owners, block, attn_width)[:, own_rows]
     gain_full = small_all[:count_seq, :gain_piece].reshape(-1).astype(jnp.float32)
     bias_wide = (
@@ -410,27 +429,10 @@
     )
     first_gain = gain_full[:D]
     second_gain = gain_full[D:]
-    pick = spread(D, own_rows, block)
     attn_mat = matmul(pick, attn_all).astype(low)
     qkv_mat = attn_mat[:, : D + 2 * KVW]
     out_mat = attn_mat[:, D + 2 * KVW :]
-
-    def by_user(flat):
-        parts = flat.reshape(own_rows, count_dp, count_seq, own_units).transpose(2, 0, 1, 3)
-        parts = jnp.pad(
-            parts, ((0, 0), (0, block - own_rows), (0, 0), (0, unit_block - own_units))
-        )
-        return parts.reshape(count_seq, block, units)
-
-    gate_up_own = jnp.concatenate([by_user(w_gate), by_user(w_up)], axis=2)
-    gate_up_own = lax.all_to_all(gate_up_own, "seq", 0, 0, tiled=True)
-    gate_up_all = lax.all_gather(
-        gate_up_own.reshape(count_seq * block, 2 * units), "dp", axis=0, tiled=True
-    )
     gate_up_mat = matmul(pick, gate_up_all).astype(low)
-    down_own = jnp.pad(w_down.reshape(own_units, D), ((0, unit_block - own_units), (0, 0)))
-    down_mat = lax.all_gather(down_own, "dp", axis=0, tiled=True)
-    grad_branch_all = lax.all_gather(out_grad.reshape(row_count, D), "seq", axis=0, tiled=True)
 
     places_all = doc_places(doc_all)
     cos_all, sin_all = rope_tables(places_all, HD)
@@ -447,6 +449,10 @@
     query_pre = qkv_pre[:, :D]
     key_value_low = qkv_pre[:, D:].astype(low).reshape(seq_count, block_len, 2 * KVW)
     key_value_all = lax.all_gather(key_value_low, "seq", axis=1, tiled=True)
+    key_value_all, grad_branch_own = lax.optimization_barrier((key_value_all, out_grad))
+    grad_branch_all = lax.all_gather(
+        grad_branch_own.reshape(row_count, D), "seq", axis=0, tiled=True
+    )
     key_all = key_value_all[..., :KVW]
     value_all = key_value_all[..., KVW:]
     key_heads = (
@@ -458,8 +464,15 @@
         0, 2, 3, 1, 4
     )
     query_rot = turn(query_heads, cos_here[:, None, None], sin_here[:, None, None]).astype(low)
-    mixed_heads, log_total = lax.map(attend_forward, (query_rot, key_rot, value_heads, allowed))
-    mixed_rows = mixed_heads.transpose(0, 3, 1, 2, 4).reshape(row_count, D).astype(low)
+    mixed_parts = []
+    log_totals = []
+    for one in range(seq_count):
+        mixed_heads, log_total = attend_forward(
+            (query_rot[one], key_rot[one], value_heads[one], allowed[one])
+        )
+        mixed_parts.append(mixed_heads.transpose(2, 0, 1, 3).reshape(block_len, D).astype(low))
+        log_totals.append(log_total)
+    mixed_rows = jnp.concatenate(mixed_parts, axis=0)
     middle = inputs + matmul(mixed_rows, out_mat)
     normed_two = rms_norm(middle, second_gain).astype(low)
 
@@ -483,42 +496,63 @@
     grad_gate_up_mat = contract_first(pick, grad_gate_up_mat).astype(low)
     grad_down_mat = contract_first(activated, grad_branch_all).astype(low)
     grad_gate_up_sum = lax.psum_scatter(grad_gate_up_mat, "dp", scatter_dimension=0, tiled=True)
-    grad_down_sum = lax.psum_scatter(grad_down_mat, "dp", scatter_dimension=0, tiled=True)
-    grad_down = grad_down_sum[:own_units].astype(jnp.float32).reshape(-1)
-    grad_gate_up_own = lax.all_to_all(
-        grad_gate_up_sum.reshape(count_seq, block, 2 * units), "seq", 0, 0, tiled=True
-    )
-    grad_gate_up_own = (
-        grad_gate_up_own[:, :own_rows]
-        .reshape(count_seq, own_rows, 2, count_dp, unit_block)[..., :own_units]
-        .transpose(2, 1, 3, 0, 4)
-        .reshape(2, -1)
-        .astype(jnp.float32)
-    )
-
     grad_result = out_grad.astype(jnp.float32).reshape(row_count, D)
     grad_middle_part, grad_second_gain = jax.vjp(rms_norm, middle, second_gain)[1](grad_normed_two)
     grad_middle = grad_result + grad_middle_part
     grad_attn = grad_middle.astype(low)
     pick_rows = lambda values: matmul(values, pick).astype(low)
     grad_out_mat = contract_first(pick_rows(mixed_rows), grad_attn).astype(low)
-    grad_out_sum = lax.psum_scatter(grad_out_mat, both, scatter_dimension=0, tiled=True)
+    grad_down_out = jnp.concatenate(
+        [
+            grad_down_mat.reshape(count_dp, unit_block, D),
+            grad_out_mat.reshape(count_dp, count_seq * block, D),
+        ],
+        axis=1,
+    ).reshape(-1, D)
+    grad_down_out = lax.psum_scatter(grad_down_out, "dp", scatter_dimension=0, tiled=True)
+    grad_down = grad_down_out[:own_units].astype(jnp.float32).reshape(-1)
+    grad_owned = jnp.concatenate([grad_gate_up_sum, grad_down_out[unit_block:]], axis=1)
+    grad_owned = lax.all_to_all(
+        grad_owned.reshape(count_seq, block, 2 * units + D), "seq", 0, 0, tiled=True
+    )
+    grad_gate_up_own = (
+        grad_owned[:, :own_rows, : 2 * units]
+        .reshape(count_seq, own_rows, 2, count_dp, unit_block)[..., :own_units]
+        .transpose(2, 1, 3, 0, 4)
+        .reshape(2, -1)
+        .astype(jnp.float32)
+    )
+    grad_out_sum = jnp.sum(grad_owned[:, :own_rows, 2 * units :].astype(jnp.float32), axis=0)
     grad_mixed = contract_last(grad_attn, out_mat).astype(low)
     grad_mixed = grad_mixed.reshape(seq_count, block_len, KVH, group_size, HD).transpose(
         0, 2, 3, 1, 4
     )
-    grad_query_rot, grad_key_rot, grad_value_heads = lax.map(
-        attend_backward, (query_rot, key_rot, value_heads, allowed, log_total, grad_mixed)
-    )
-    grad_query_pre = unturn(grad_query_rot, cos_here[:, None, None], sin_here[:, None, None])
-    grad_query_low = grad_query_pre.transpose(0, 3, 1, 2, 4).reshape(row_count, D).astype(low)
-    grad_key_all = (
-        unturn(grad_key_rot, cos_all[:, None], sin_all[:, None])
-        .transpose(0, 2, 1, 3)
-        .reshape(seq_count, seq_len, KVW)
-    )
-    grad_value_all = grad_value_heads.transpose(0, 2, 1, 3).reshape(seq_count, seq_len, KVW)
-    grad_key_value = jnp.concatenate([grad_key_all, grad_value_all], axis=-1).astype(low)
+    grad_query_parts = []
+    grad_key_value_parts = []
+    for one in range(seq_count):
+        grad_query_rot, grad_key_rot, grad_value_heads = attend_backward(
+            (
+                query_rot[one],
+                key_rot[one],
+                value_heads[one],
+                allowed[one],
+                log_totals[one],
+                grad_mixed[one],
+            )
+        )
+        grad_query_pre = unturn(grad_query_rot, cos_here[one], sin_here[one])
+        grad_query_parts.append(
+            grad_query_pre.transpose(2, 0, 1, 3).reshape(block_len, D).astype(low)
+        )
+        grad_key_pre = unturn(grad_key_rot, cos_all[one], sin_all[one])
+        grad_key_value_parts.append(
+            jnp.concatenate([grad_key_pre, grad_value_heads], axis=0)
+            .transpose(1, 0, 2)
+            .reshape(seq_len, 2 * KVW)
+            .astype(low)
+        )
+    grad_query_low = jnp.concatenate(grad_query_parts, axis=0)
+    grad_key_value = jnp.stack(grad_key_value_parts)
     grad_key_value_low = lax.psum_scatter(
         grad_key_value, "seq", scatter_dimension=1, tiled=True
     ).reshape(row_count, 2 * KVW)
@@ -529,19 +563,35 @@
     input_grad = (grad_middle + grad_inputs_part).reshape(seq_count, block_len, D)
     gain_total = jnp.concatenate([grad_first_gain, grad_second_gain]).reshape(count_seq, gain_piece)
     bias_total = jnp.sum(grad_qkv_low.astype(jnp.float32), axis=0).reshape(count_seq, bias_piece)
-    gain_sum, bias_sum = lax.psum((gain_total, bias_total), both)
-    gain_grad = lax.dynamic_slice_in_dim(gain_sum, seq_index, 1, 0).reshape(-1)
-    bias_grad = lax.dynamic_slice_in_dim(bias_sum, seq_index, 1, 0).reshape(-1)
-    grad_qkv_sum = lax.psum_scatter(
-        grad_qkv_mat.astype(low), both, scatter_dimension=0, tiled=True
-    )[:own_rows].astype(jnp.float32)
+    small_total = jnp.concatenate([gain_total, bias_total], axis=1)
+    small_total = jnp.tile(small_total, (count_dp, 1))[:, None]
+    qkv_width = D + 2 * KVW
+    small_total = jnp.pad(
+        small_total,
+        (
+            (0, 0),
+            (own_rows, block - own_rows - 1),
+            (0, qkv_width - gain_piece - bias_piece),
+        ),
+    )
+    grad_qkv_mat = grad_qkv_mat + small_total.reshape(owners * block, qkv_width)
+    grad_qkv_part = lax.psum_scatter(
+        grad_qkv_mat.astype(low), "dp", scatter_dimension=0, tiled=True
+    )
+    grad_qkv_part = lax.all_to_all(
+        grad_qkv_part.reshape(count_seq, block, qkv_width), "seq", 0, 0, tiled=True
+    )
+    grad_qkv_sum = jnp.sum(grad_qkv_part.astype(jnp.float32), axis=0)
+    gain_grad = grad_qkv_sum[own_rows, :gain_piece]
+    bias_grad = grad_qkv_sum[own_rows, gain_piece : gain_piece + bias_piece]
+    grad_qkv_sum = grad_qkv_sum[:own_rows]
     return (
         output,
         input_grad,
         grad_qkv_sum[:, :D].reshape(-1),
         grad_qkv_sum[:, D : D + KVW].reshape(-1),
         grad_qkv_sum[:, D + KVW :].reshape(-1),
-        grad_out_sum[:own_rows].astype(jnp.float32).reshape(-1),
+        grad_out_sum.reshape(-1),
         grad_gate_up_own[0],
         grad_gate_up_own[1],
         grad_down,

time: 768 us -> 614 us (0.80)
  waiting for transfers between devices: 490 us -> 343 us
  local copies, waits for them, and re-layouts: 60.8 us -> 44.3 us
  blocking collectives: 39.7 us -> 28.6 us
  starting transfers between devices: 8.88 us -> 19.6 us
  matrix products: 108 us -> 117 us
    reduce_scatter x3 -> x2, waiting for transfers between devices: 211 us -> 48.7 us  [the longest x1 41.1 us: shards_split(): lax.psum_scatter(grad_down_out, 'dp', scatter_dimension=0, tiled=True)]
    all_gather x1, waiting for transfers between devices: 63.1 us -> 0.01 us  [shards_split(): attn_all = lax.all_gather(attn_rows, both, axis=0, tiled=True)]
    reduce_scatter x1, waiting for transfers between devices: 0.02 us -> 41.3 us  [shards_split(): lax.psum_scatter(grad_gate_up_mat, 'dp', scatter_dimension=0, tiled=True)]
    all_to_all x2 -> x4, waiting for transfers between devices: 23.7 us -> 64.1 us  [the longest x2 43 us: to_all_dp(): lax.all_to_all(copies, 'dp', 0, 0, tiled=True).reshape(-1, piece.shape[1])]
    psum x1 -> x0, blocking collectives: 39.7 us -> none  [shards_split(): gain_sum, bias_sum = lax.psum((gain_total, bias_total), both)]
    all_gather x3 -> x1, waiting for transfers between devices: 66.7 us -> 32.1 us  [shards_split(): lax.all_gather(grad_branch_own.reshape(row_count, D), 'seq', axis=0, tile...]
    all_to_all x0 -> x1, blocking collectives: none -> 28.6 us  [shards_split(): gate_up_own = lax.all_to_all(gate_up_own, 'seq', 0, 0, tiled=True)]
    dynamic_update_slice x2 -> x0, local copies, waits for them, and re-layouts: 23.2 us -> none  [shards_split(): lax.map(attend_forward, (query_rot, key_rot, value_heads, allowed))]
  transfers between devices with their start and end apart: 15 -> 14, of which waited for: 12 -> 12; matrix products, arithmetic and copies ran while one was open for 21% -> 14% of each run, Pallas kernels for 0% -> 0%
where the time goes in v2:
time: 614 us; the launch traced here: 606 us
  waiting for transfers between devices  343 us (56%)
  matrix products  117 us (19%)
  local copies, waits for them, and re-layouts  44.3 us (7%)
  other arithmetic  37.7 us (6%)
  blocking collectives  28.6 us (5%)
  starting transfers between devices  19.6 us (3%)
  between operations  15.9 us (3%)
    reduce_scatter x1, waiting for transfers between devices, shards_split(): lax.psum_scatter(branch_part, 'seq', scatter_dimension=0, tiled=True)  44.3 us
    all_to_all x2, waiting for transfers between devices, to_all_dp(): lax.all_to_all(copies, 'dp', 0, 0, tiled=True).reshape(-1, piece.shape[1])  43 us
    reduce_scatter x1, waiting for transfers between devices, shards_split(): lax.psum_scatter(grad_gate_up_mat, 'dp', scatter_dimension=0, tiled=True)  41.3 us
    reduce_scatter x1, waiting for transfers between devices, shards_split(): lax.psum_scatter(grad_down_out, 'dp', scatter_dimension=0, tiled=True)  41.1 us
    dot_general x6, matrix products, matmul(): return jnp.dot(left, right, preferred_element_type=jnp.float32)  36.1 us
    all_gather x1, waiting for transfers between devices, shards_split(): normed_all = lax.all_gather(normed_two, 'seq', axis=0, tiled=True)  35.9 us
    reduce_scatter x1, waiting for transfers between devices, shards_split(): lax.psum_scatter(grad_normed_part, 'seq', scatter_dimension=0, tiled=True)  35.8 us
    all_gather x1, waiting for transfers between devices, shards_split(): lax.all_gather(grad_branch_own.reshape(row_count, D), 'seq', axis=0, tile...  32.1 us
  transfers between devices with their start and end apart: 14, of which 12 were waited for; matrix products, arithmetic and copies ran while one was open for 14% of the time, Pallas kernels for 0%

profile of v2, /device:TPU:0, one launch (start us, length us, event | category | flops | bytes accessed | tf_op | source)
XLA Modules:
  0.0 606.1 jit_solution(13997772445791206995)
XLA Ops:
  10.6 1.5 maximum_maximum_fusion
  14.5 5.2 all-to-all-start.2
  19.6 1.3 reshape.373
  21.7 1.3 reshape.375
  23.9 11.4 %all-to-all-done.2 = bf16[4,160,896]{2,1,0:T(8,128)(2,1)S(1)} async-done(((bf16[4,160,896]{2,1,0:T(8,128)(2,1)}), bf16[4,160,896]{2,1,0:T(8,128)(2,1)S(1)}, u32[]{:S(2)}, u32[]{:S(2)}) %all-to-all-start.2) | async-done | bytes 1146912 | tf_op jit(solution)/shard_map/all_to_all | solution.py:402
  35.3 28.6 %all_to_all.25 = bf16[8,32,1280]{2,1,0:T(8,128)(2,1)S(1)} all-to-all(bf16[8,32,1280]{2,1,0:T(8,128)(2,1)S(1)} %pad_maximum_fusion.8), channel_id=1, replica_groups=mesh['dp'=4,'seq'=8] {'seq'}, dimensions={0} | all-to-all | bytes 1310720 | tf_op jit(solution)/shard_map/all_to_all | solution.py:412
  63.8 1.7 broadcast_in_dim.45
  65.5 3.7 all-to-all-start.1
  70.8 31.6 %all-to-all-done.1 = bf16[4,256,1280]{2,1,0:T(8,128)(2,1)S(1)} async-done(((bf16[4,256,1280]{2,1,0:T(8,128)(2,1)}), bf16[4,256,1280]{2,1,0:T(8,128)(2,1)S(1)}, u32[]{:S(2)}, u32[]{:S(2)}) %all-to-all-start.1) | async-done | bytes 2621472 | tf_op jit(solution)/shard_map/all_to_all | solution.py:402
  102.4 2.3 slice.247
  105.1 7.7 %fusion.21 = bf16[896,2048]{1,0:T(8,128)(2,1)} fusion(bf16[1024,2048]{1,0:T(8,128)(2,1)} %all-gather.5.cloned.1.call-done, s32[896]{0:T(1024)S(1)} %fusion.106), kind=kOutput, calls=%fused_computation.39 | convolution fusion | flops 3760848896 | bytes 7867904 | tf_op jit(solution)/shard_map/dot_general | solution.py:62
  113.9 2.4 convolution_add_fusion.1
  119.0 1.6 multiply_cosine_fusion
  124.8 14.5 %all-gather.7.cloned.1.call-done = bf16[2,1024,256]{2,1,0:T(8,128)(2,1)} async-done(((bf16[2,128,256]{2,1,0:T(8,128)(2,1)}), bf16[2,1024,256]{2,1,0:T(8,128)(2,1)}) %all-gather.7.cloned.1.call-update) | async-done | bytes 1048592 | tf_op jit(solution)/shard_map/all_gather | solution.py:451
  139.3 2.1 fusion.118
  144.0 1.9 fusion.60
  145.9 1.4 fusion.125
  147.4 1.4 fusion.124
  148.8 1.6 fusion
  150.4 2.1 fusion.56
  152.5 1.6 fusion.1
  154.2 1.8 fusion.55
  156.1 2.3 multiply_reduce_fusion.3
  160.0 5.9 fusion.22
  165.9 35.9 %all-gather.9.cloned.1.call-done = bf16[2048,896]{1,0:T(8,128)(2,1)} async-done(((bf16[256,896]{1,0:T(8,128)(2,1)}), bf16[2048,896]{1,0:T(8,128)(2,1)}) %all-gather.9.cloned.1.call-update) | async-done | bytes 3670032 | tf_op jit(solution)/shard_map/all_gather | solution.py:479
  201.8 10.9 %fusion.126 = f32[2048,1280]{0,1:T(8,128)} fusion(bf16[2048,896]{1,0:T(8,128)(2,1)} %all-gather.9.cloned.1.call-done, bf16[896,1280]{1,0:T(8,128)(2,1)} %fusion.22), kind=kOutput, calls=%fused_computation.247 | convolution fusion | flops 4697620480 | bytes 16449536 | tf_op jit(solution)/shard_map/dot_general | solution.py:62
  212.7 32.1 %all-gather.11.cloned.1.call-done = bf16[2048,896]{1,0:T(8,128)(2,1)} async-done(((bf16[256,896]{1,0:T(8,128)(2,1)}), bf16[2048,896]{1,0:T(8,128)(2,1)}) %all-gather.11.cloned.1.call-update) | async-done | bytes 3670032 | tf_op jit(solution)/shard_map/all_gather | solution.py:453
  244.8 9.6 %fusion.6 = (bf16[2048,640]{0,1:T(8,128)(2,1)S(1)}, bf16[2048,640]{0,1:T(8,128)(2,1)S(1)}, bf16[2048,640]{0,1:T(8,128)(2,1)}) fusion(f32[2048,1280]{0,1:T(8,128)} %fusion.126, bf16[2048,896]{1,0:T(8,128)(2,1)} %all-gather.11.cloned.1.call-done, bf16[640,896]{1,0:T(8,128)(2,1)S(1)} %bitcast.263), kind=kOutput, calls=%fused_computation.19 | convolution fusion | flops 2369781760 | bytes 23166976 | tf_op jit(solution)/shard_map/dot_general | solution.py:66
  254.4 1.5 copy-done.49
  256.8 7.1 %convolution_convert_fusion.2 = bf16[2048,896]{1,0:T(8,128)(2,1)} fusion(bf16[896,1280]{1,0:T(8,128)(2,1)S(1)} %copy-done.48, bf16[2048,640]{0,1:T(8,128)(2,1)S(1)} %get-tuple-element.26, bf16[2048,640]{0,1:T(8,128)(2,1)S(1)} %get-tuple-element.25), kind=kOutput, calls=%fused_computation.42 | convolution fusion | flops 4709941248 | bytes 11206656 | tf_op jit(solution)/shard_map/dot_general | solution.py:66
  263.9 6.9 %convolution_convert_fusion.3 = bf16[2048,896]{1,0:T(8,128)(2,1)} fusion(bf16[2048,640]{0,1:T(8,128)(2,1)} %get-tuple-element.27, bf16[640,896]{1,0:T(8,128)(2,1)S(1)} %bitcast.264), kind=kOutput, calls=%fused_computation.43 | convolution fusion | flops 2350645248 | bytes 7438336 | tf_op jit(solution)/shard_map/dot_general | solution.py:62
  272.1 35.8 %reduce-scatter.11.cloned.1.call-done = bf16[256,896]{1,0:T(8,128)(2,1)} async-done(((bf16[2048,896]{1,0:T(8,128)(2,1)}), bf16[256,896]{1,0:T(8,128)(2,1)}) %reduce-scatter.11.cloned.1.call-update) | async-done | bytes 458768 | tf_op jit(solution)/shard_map/reduce_scatter | solution.py:488
  308.0 1.3 fusion.62
  309.3 44.3 %reduce-scatter.9.cloned.1.call-done = bf16[256,896]{1,0:T(8,128)(2,1)} async-done(((bf16[2048,896]{1,0:T(8,128)(2,1)}), bf16[256,896]{1,0:T(8,128)(2,1)}) %reduce-scatter.9.cloned.1.call-update) | async-done | bytes 458768 | tf_op jit(solution)/shard_map/reduce_scatter | solution.py:492
  353.6 2.3 fusion.63
  356.8 2.9 fusion.40
  359.7 2.7 reshape.424
  362.5 2.7 copy.82
  365.1 5.4 multiply_reduce_fusion.1
  370.6 5.3 fusion.52
  375.9 2.0 multiply_reduce_fusion
  377.9 1.3 fusion.49
  379.3 1.6 multiply_convert_fusion.1
  380.9 2.0 broadcast_multiply_fusion.1
  383.0 1.6 multiply_convert_fusion
  389.4 3.4 broadcast_multiply_fusion.3
  394.3 25.5 %reduce-scatter.19.cloned.1.call-done = bf16[128,512]{1,0:T(8,128)(2,1)} async-done(((bf16[1024,512]{1,0:T(8,128)(2,1)}), bf16[128,512]{1,0:T(8,128)(2,1)}) %reduce-scatter.19.cloned.1.call-update) | async-done | bytes 131088
  421.2 3.5 multiply_reduce_fusion.2
  424.9 2.7 pad.23
  427.7 5.5 fusion.8
  433.3 6.8 %convolution_convert_fusion.5 = bf16[640,896]{1,0:T(8,128)(2,1)} fusion(bf16[2048,640]{0,1:T(8,128)(2,1)} %get-tuple-element.27, bf16[2048,896]{1,0:T(8,128)(2,1)} %all-gather.11.cloned.1.call-done), kind=kOutput, calls=%fused_computation.56 | convolution fusion | flops 2349383680 | bytes 7438336 | tf_op jit(solution)/shard_map/dot_general | solution.py:72
  440.1 2.8 convolution_convert_fusion.4
  442.9 3.7 pad_maximum_fusion.3
  446.9 14.4 %convolution_convert_fusion = bf16[1024,1280]{1,0:T(8,128)(2,1)} fusion(s32[896]{0:T(1024)S(1)} %copy-done.39, bf16[2048,896]{1,0:T(8,128)(2,1)} %all-gather.9.cloned.1.call-done, bf16[2048,640]{0,1:T(8,128)(2,1)} %copy-done.50, bf16[2048,640]{0,1:T(8,128)(2,1)} %copy-done.49), kind=kOutput, calls=%fused_computation.27 | convolution fusion | flops 7060291584 | bytes 11537920 | tf_op jit(solution)/shard_map/dot_general | solution.py:72
  461.4 7.6 %reduce-scatter.13.cloned.1.call-done = bf16[256,1152]{1,0:T(8,128)(2,1)} async-done(((bf16[1024,1152]{1,0:T(8,128)(2,1)}), bf16[256,1152]{1,0:T(8,128)(2,1)}) %reduce-scatter.13.cloned.1.call-update) | async-done | bytes 589840 | tf_op jit(solution)/shard_map/reduce_scatter | solution.py:578
  469.0 4.6 all-to-all-start.3
  473.6 41.1 %reduce-scatter.17.cloned.1.call-done = bf16[416,896]{1,0:T(8,128)(2,1)} async-done(((bf16[1664,896]{1,0:T(8,128)(2,1)}), bf16[416,896]{1,0:T(8,128)(2,1)}) %reduce-scatter.17.cloned.1.call-update) | async-done | bytes 745488 | tf_op jit(solution)/shard_map/reduce_scatter | solution.py:512
  515.8 41.3 %reduce-scatter.15.cloned.1.call-done = bf16[256,1280]{1,0:T(8,128)(2,1)} async-done(((bf16[1024,1280]{1,0:T(8,128)(2,1)}), bf16[256,1280]{1,0:T(8,128)(2,1)}) %reduce-scatter.15.cloned.1.call-update) | async-done | bytes 655376 | tf_op jit(solution)/shard_map/reduce_scatter | solution.py:498
  557.1 2.2 pad_maximum_fusion.4
  559.4 4.9 all-to-all-start.4
  564.3 2.4 fusion.64
  571.1 21.2 %all-to-all-done.4 = bf16[8,32,2176]{2,1,0:T(8,128)(2,1)S(1)} async-done(((bf16[8,32,2176]{2,1,0:T(8,128)(2,1)}), bf16[8,32,2176]{2,1,0:T(8,128)(2,1)S(1)}, u32[]{:S(2)}, u32[]{:S(2)}) %all-to-all-start.4) | async-done | bytes 1114144 | tf_op jit(solution)/shard_map/all_to_all | solution.py:515
  594.5 1.7 squeeze.64
  596.3 1.7 squeeze.65
  (236 shorter events, 41.1 us)
Async XLA Ops:
  7.2 12.5 %copy-start.35 = (bf16[136192]{0:T(1024)(128)(2,1)S(1)}, bf16[136192]{0:T(1024)(128)(2,1)}, u32[]{:S(2)}) copy-start(bf16[136192]{0:T(1024)(128)(2,1)} %param.18) | copy-start | bytes 817156
  7.2 95.2 %all-gather.5.cloned.1.call-start = ((), (), s32[]{:S(2)}) async-start(), calls=%async_computation.11 | async-start | bytes 4325376 | tf_op jit(solution)/shard_map/all_gather | solution.py:397
  13.3 8.4 %copy-start.36 = (bf16[136192]{0:T(1024)(128)(2,1)S(1)}, bf16[136192]{0:T(1024)(128)(2,1)}, u32[]{:S(2)}) copy-start(bf16[136192]{0:T(1024)(128)(2,1)} %param.19) | copy-start | bytes 817156
  14.5 20.8 %all-to-all-start.2 = ((bf16[4,160,896]{2,1,0:T(8,128)(2,1)}), bf16[4,160,896]{2,1,0:T(8,128)(2,1)S(1)}, u32[]{:S(2)}, u32[]{:S(2)}) async-start(bf16[4,160,896]{2,1,0:T(8,128)(2,1)} %broadcast_in_dim.46), calls=%async_computation.2 | async-start | bytes 2293760 | tf_op jit(solution)/shard_map/all_to_all | solution.py:402
  35.3 30.2 %copy-start.26 = (bf16[4,160,896]{2,1,0:T(8,128)(2,1)}, bf16[4,160,896]{2,1,0:T(8,128)(2,1)S(1)}, u32[]{:S(2)}) copy-start(bf16[4,160,896]{2,1,0:T(8,128)(2,1)S(1)} %all-to-all-done.2) | copy-start | bytes 3440644
  63.8 5.9 copy-start.8
  65.5 36.9 %all-to-all-start.1 = ((bf16[4,256,1280]{2,1,0:T(8,128)(2,1)}), bf16[4,256,1280]{2,1,0:T(8,128)(2,1)S(1)}, u32[]{:S(2)}, u32[]{:S(2)}) async-start(bf16[4,256,1280]{2,1,0:T(8,128)(2,1)} %broadcast_in_dim.45), calls=%async_computation.1 | async-start | bytes 5242880 | tf_op jit(solution)/shard_map/all_to_all | solution.py:402
  69.2 70.1 %all-gather.7.cloned.1.call-start = ((), (), s32[]{:S(2)}) async-start(), calls=%async_computation.12 | async-start | bytes 1179648 | tf_op jit(solution)/shard_map/all_gather | solution.py:451
  69.8 43.1 %copy-start.37 = (s32[896]{0:T(1024)}, s32[896]{0:T(1024)S(1)}, u32[]{:S(2)}) copy-start(s32[896]{0:T(1024)S(1)} %fusion.106) | copy-start | bytes 10756
  70.0 34.8 %copy-start.40 = (f32[2,128]{1,0:T(2,128)}, f32[2,128]{1,0:T(2,128)S(1)}, u32[]{:S(2)}) copy-start(f32[2,128]{1,0:T(2,128)S(1)} %multiply_reduce_fusion.4) | copy-start | bytes 3076
  70.0 42.9 %copy-start.42 = (f32[256]{0:T(256)}, f32[256]{0:T(256)S(1)}, u32[]{:S(2)}) copy-start(f32[256]{0:T(256)S(1)} %bitcast_rsqrt_fusion) | copy-start | bytes 3076
  102.4 10.5 %copy-start.15 = (bf16[4,256,1280]{2,1,0:T(8,128)(2,1)}, bf16[4,256,1280]{2,1,0:T(8,128)(2,1)S(1)}, u32[]{:S(2)}) copy-start(bf16[4,256,1280]{2,1,0:T(8,128)(2,1)S(1)} %all-to-all-done.1) | copy-start | bytes 7864324
  117.0 84.8 %all-gather.9.cloned.1.call-start = ((), (), s32[]{:S(2)}) async-start(), calls=%async_computation.13 | async-start | bytes 4128768 | tf_op jit(solution)/shard_map/all_gather | solution.py:479
  120.7 3.1 copy-start.31
  120.7 3.1 copy-start.33
  124.8 19.3 %copy-start.20 = (f32[2,1024,64]{1,2,0:T(8,128)S(1)}, f32[2,1024,64]{1,2,0:T(8,128)}, u32[]{:S(2)}) copy-start(f32[2,1024,64]{1,2,0:T(8,128)} %get-tuple-element.81) | copy-start | bytes 1572868
  141.7 4.2 copy-start.11
  141.7 4.2 copy-start.25
  144.0 10.2 %copy-start.18 = (bf16[2,1024,128]{1,2,0:T(8,128)(2,1)}, bf16[2,1024,128]{1,2,0:T(8,128)(2,1)S(1)}, u32[]{:S(2)}) copy-start(bf16[2,1024,128]{1,2,0:T(8,128)(2,1)S(1)} %copy.80) | copy-start | bytes 1572868
  147.3 3.1 copy-start.1
  148.8 5.4 copy-start
  152.5 3.5 copy-start.44
  154.2 1.9 copy-start.9
  156.1 9.8 %copy-start.46 = (bf16[2,7,128,64]{2,3,1,0:T(8,128)(2,1)}, bf16[2,7,128,64]{2,3,1,0:T(8,128)(2,1)S(1)}, u32[]{:S(2)}) copy-start(bf16[2,7,128,64]{2,3,1,0:T(8,128)(2,1)S(1)} %fusion.55) | copy-start | bytes 688132
  156.1 3.9 copy-start.38
  159.4 85.4 %all-gather.11.cloned.1.call-start = ((), (), s32[]{:S(2)}) async-start(), calls=%async_computation.15 | async-start | bytes 4128768 | tf_op jit(solution)/shard_map/all_gather | solution.py:453
  160.0 148.0 %reduce-scatter.11.cloned.1.call-start = ((), (), s32[]{:S(2)}) async-start(), calls=%async_computation.16 | async-start | bytes 4128768 | tf_op jit(solution)/shard_map/reduce_scatter | solution.py:488
  165.9 78.9 %copy-start.27 = (bf16[4,160,896]{2,1,0:T(8,128)(2,1)S(1)}, bf16[4,160,896]{2,1,0:T(8,128)(2,1)}, u32[]{:S(2)}) copy-start(bf16[4,160,896]{2,1,0:T(8,128)(2,1)} %copy-done.26) | copy-start | bytes 3440644
  244.8 12.0 %copy-start.48 = (bf16[896,1280]{1,0:T(8,128)(2,1)S(1)}, bf16[896,1280]{1,0:T(8,128)(2,1)}, u32[]{:S(2)}) copy-start(bf16[896,1280]{1,0:T(8,128)(2,1)} %fusion.22) | copy-start | bytes 6881284
  254.4 1.5 copy-start.49
  254.4 2.4 copy-start.50
  263.9 89.7 %reduce-scatter.9.cloned.1.call-start = ((), (), s32[]{:S(2)}) async-start(), calls=%async_computation.14 | async-start | bytes 4128768 | tf_op jit(solution)/shard_map/reduce_scatter | solution.py:492
  270.8 82.8 %copy-start.21 = (bf16[2,128,896]{2,1,0:T(8,128)(2,1)S(1)}, bf16[2,128,896]{2,1,0:T(8,128)(2,1)}, u32[]{:S(2)}) copy-start(bf16[2,128,896]{2,1,0:T(8,128)(2,1)} %param.23) | copy-start | bytes 1376260
  270.9 148.9 %reduce-scatter.19.cloned.1.call-start = ((), (), s32[]{:S(2)}) async-start(), calls=%async_computation.20 | async-start | bytes 1179648
  359.7 16.1 %slice-start = ((s8[7340032]{0:T(1024)(128)(4,1)}), s8[3145728]{0:T(1024)(128)(4,1)S(1)}, s32[]{:S(2)}) async-start(s8[7340032]{0:T(1024)(128)(4,1)} %bitcast.229), calls=%async_computation.21 | async-start | bytes 6291456
  365.1 5.4 copy-start.7
  365.1 10.7 %slice-start.1 = ((s8[7340032]{0:T(1024)(128)(4,1)}), s8[4194304]{0:T(1024)(128)(4,1)S(1)}, s32[]{:S(2)}) async-start(s8[7340032]{0:T(1024)(128)(4,1)} %bitcast.229), calls=%async_computation.22 | async-start | bytes 8388608
  370.5 5.3 copy-start.19
  370.6 8.7 %slice-start.2 = ((s8[7340032]{0:T(1024)(128)(4,1)}), s8[4194304]{0:T(1024)(128)(4,1)S(1)}, s32[]{:S(2)}) async-start(s8[7340032]{0:T(1024)(128)(4,1)} %bitcast.231), calls=%async_computation.23 | async-start | bytes 8388608
  375.9 3.4 slice-start.3
  379.3 1.6 copy-start.17
  380.9 3.7 copy-start.2
  382.9 1.7 copy-start.12
  382.9 1.7 copy-start.16
  384.6 1.8 copy-start.3
  384.6 1.8 copy-start.28
  384.6 1.8 copy-start.29
  386.6 2.6 copy-start.34
  386.6 2.6 copy-start.32
  386.6 2.7 copy-start.6
  388.9 80.1 %reduce-scatter.13.cloned.1.call-start = ((), (), s32[]{:S(2)}) async-start(), calls=%async_computation.17 | async-start | bytes 2949120 | tf_op jit(solution)/shard_map/reduce_scatter | solution.py:578
  389.3 3.5 copy-start.4
  392.8 28.3 %copy-start.10 = (bf16[2,128,896]{2,1,0:T(8,128)(2,1)S(1)}, bf16[2,128,896]{2,1,0:T(8,128)(2,1)}, u32[]{:S(2)}) copy-start(bf16[2,128,896]{2,1,0:T(8,128)(2,1)} %param.12) | copy-start | bytes 1376260
  392.8 28.3 %copy-start.43 = (f32[256]{0:T(256)S(1)}, f32[256]{0:T(256)}, u32[]{:S(2)}) copy-start(f32[256]{0:T(256)} %copy-done.42) | copy-start | bytes 3076
  424.6 3.1 copy-start.23
  424.6 3.1 copy-start.39
  433.2 6.9 %copy-start.14 = (f32[256,896]{1,0:T(8,128)S(1)}, f32[256,896]{1,0:T(8,128)}, u32[]{:S(2)}) copy-start(f32[256,896]{1,0:T(8,128)} %copy-done.13) | copy-start | bytes 2752516
  433.2 6.9 %copy-start.45 = (bf16[2,7,128,64]{2,3,1,0:T(8,128)(2,1)S(1)}, bf16[2,7,128,64]{2,3,1,0:T(8,128)(2,1)}, u32[]{:S(2)}) copy-start(bf16[2,7,128,64]{2,3,1,0:T(8,128)(2,1)} %copy-done.44) | copy-start | bytes 688132
  433.3 6.9 %copy-start.47 = (bf16[2,7,128,64]{2,3,1,0:T(8,128)(2,1)S(1)}, bf16[2,7,128,64]{2,3,1,0:T(8,128)(2,1)}, u32[]{:S(2)}) copy-start(bf16[2,7,128,64]{2,3,1,0:T(8,128)(2,1)} %copy-done.46) | copy-start | bytes 688132
  433.3 81.4 %reduce-scatter.17.cloned.1.call-start = ((), (), s32[]{:S(2)}) async-start(), calls=%async_computation.19 | async-start | bytes 3727360 | tf_op jit(solution)/shard_map/reduce_scatter | solution.py:512
  446.6 110.5 %reduce-scatter.15.cloned.1.call-start = ((), (), s32[]{:S(2)}) async-start(), calls=%async_computation.18 | async-start | bytes 3276800 | tf_op jit(solution)/shard_map/reduce_scatter | solution.py:498
  461.4 102.9 %copy-start.41 = (f32[2,128]{1,0:T(2,128)S(1)}, f32[2,128]{1,0:T(2,128)}, u32[]{:S(2)}) copy-start(f32[2,128]{1,0:T(2,128)} %copy-done.40) | copy-start | bytes 3076
  469.0 90.4 %all-to-all-start.3 = ((bf16[8,32,1152]{2,1,0:T(8,128)(2,1)}), bf16[8,32,1152]{2,1,0:T(8,128)(2,1)S(1)}, u32[]{:S(2)}, u32[]{:S(2)}) async-start(bf16[8,32,1152]{2,1,0:T(8,128)(2,1)} %bitcast.267), calls=%async_computation.6 | async-start | bytes 1179648 | tf_op jit(solution)/shard_map/all_to_all | solution.py:581
  559.4 32.9 %all-to-all-start.4 = ((bf16[8,32,2176]{2,1,0:T(8,128)(2,1)}), bf16[8,32,2176]{2,1,0:T(8,128)(2,1)S(1)}, u32[]{:S(2)}, u32[]{:S(2)}) async-start(bf16[8,32,2176]{2,1,0:T(8,128)(2,1)} %bitcast.84), calls=%async_computation.9 | async-start | bytes 2228224 | tf_op jit(solution)/shard_map/all_to_all | solution.py:515
  (5 other events, 5.7 us)
Sparse Core Ops, SparseCore 0:
  12.2 89.1 all-gather.4
  117.1 22.0 all-gather.6
  159.5 42.2 all-gather.8
  203.3 41.4 all-gather.10
  264.0 43.9 reduce-scatter.10
  310.1 43.4 reduce-scatter.8
  389.1 30.7 reduce-scatter.18
  433.4 35.5 reduce-scatter.12
  472.1 42.5 reduce-scatter.16
  517.5 39.5 reduce-scatter.14
